TPU v7x, 32 devices: a whole 2x2x4 slice. The times are simulated.
32 devices in a mesh: seq: 8 (over y, x, core), chan: 4 (over z).
Axes of the slice: x: 2, y: 2, z: 4, core: 2. Of those that a mesh axis runs over, the one named last changes fastest.
Arguments:
- doc_ids: int32 [2048], replicated, may hold values from 0 to 3, never falling along the last dimension, each value on 1 to 1024 neighbouring positions
- attn_queries: bfloat16 [2048, 8192], P(('seq', 'chan')), may hold values from -6 to 6
- attn_keys: bfloat16 [2048, 8192], P(('seq', 'chan')), may hold values from -6 to 6
- attn_values: bfloat16 [2048, 8192], P(('seq', 'chan')), may hold values from -6 to 6
- attn_cot: bfloat16 [2048, 8192], P(('seq', 'chan')), may hold values from -6 to 6
Outputs:
- attn_out: bfloat16 [2048, 8192], P('seq', 'chan')
- query_grad: bfloat16 [2048, 8192], P('seq', 'chan')
- key_grad: bfloat16 [2048, 8192], P('seq', 'chan')
- value_grad: bfloat16 [2048, 8192], P('seq', 'chan')
Inputs may be any that keep to these rules, and one draw needn't show every extreme that they name: `doc_ids`: documents are runs of equal ids that never fall; each holds 1 to 1024 tokens and one holds exactly 1024.
All inputs are finite; a program needn't handle non-finite values.
Results may differ from a plain program's by a relative error of at most 0.03.
Values may be sent and summed in bfloat16 or wider, within the bound.
No kernel may reach another device: no remote copies, remote signals or barrier semaphores. Data moves between devices by JAX's collectives and lax.ppermute only.
A program may use at most 256 MiB of HBM per device.

v0:
```python
import functools
import math

import jax
import jax.numpy as jnp
from jax import lax
from jax.experimental import pallas as pl
from jax.experimental.pallas import tpu as pltpu
from jax.sharding import PartitionSpec as P

HEAD_DIM = 128
DOC_MAX = 1024
NEG = -1e30
SCALE = HEAD_DIM ** (-0.5)
EXP_SCALE = SCALE * math.log2(math.e)
SCALARS = pl.BlockSpec(memory_space=pltpu.SMEM)
VECTORS = pl.BlockSpec(memory_space=pltpu.VMEM)
ANYWHERE = pl.BlockSpec(memory_space=pl.ANY)


def low_array(*shape):
    return jax.ShapeDtypeStruct(shape, jnp.bfloat16)


def moved(byte_count):
    return pl.CostEstimate(flops=0, bytes_accessed=byte_count, transcendentals=0)


def dot_nt(a, b):
    return lax.dot_general(a, b, (((1,), (1,)), ((), ())), preferred_element_type=jnp.float32)


def dot_nn(a, b):
    return lax.dot_general(a, b, (((1,), (0,)), ((), ())), preferred_element_type=jnp.float32)


def dot_tn(a, b):
    return lax.dot_general(a, b, (((0,), (0,)), ((), ())), preferred_element_type=jnp.float32)


def pack_kernel(group, size, place_ref, *refs):
    query, key, value, cot, out_ref = refs
    core = place_ref[0]
    for chip in range(group):
        for j in range(size):
            columns = slice((chip * size + j) * HEAD_DIM, (chip * size + j + 1) * HEAD_DIM)
            out_ref[2 * chip + core, 0, j, 0] = query[:, columns]
            out_ref[2 * chip + core, 0, j, 1] = cot[:, columns]
            out_ref[2 * chip + 1 - core, 0, j, 0] = key[:, columns]
            out_ref[2 * chip + 1 - core, 0, j, 1] = value[:, columns]


def pack(place, inputs, chans, group, offset, size):
    rows, width = inputs[0].shape
    part = group * size * HEAD_DIM
    per_chan = width // chans // part
    return pl.pallas_call(
        functools.partial(pack_kernel, group, size),
        grid=(chans,),
        out_shape=low_array(2 * group, chans, size, 2, rows, HEAD_DIM),
        in_specs=[SCALARS]
        + [pl.BlockSpec((rows, part), lambda c: (0, c * per_chan + offset // size))] * 4,
        out_specs=pl.BlockSpec(
            (2 * group, 1, size, 2, rows, HEAD_DIM), lambda c: (0, c, 0, 0, 0, 0)
        ),
        cost_estimate=moved(16 * rows * part * chans),
    )(place, *inputs)


def attention_kernel(spans, size, group, *refs):
    count_ref, place_ref, start_ref, mine_ref, other_ref = refs[:5]
    outs, (keep_ref, send_ref) = refs[5 : 5 + group], refs[5 + group : 7 + group]
    pair_ref, key_ref, mixed_ref, key_acc, value_acc, load_sems, sems = refs[7 + group :]
    block = mixed_ref.shape[3]
    core = place_ref[0]
    loads = []
    for j in range(size):
        for m in range(group):
            same, cross = 2 * m + core, 2 * m + 1 - core
            sem = load_sems.at[j, m]
            for k, (source, target) in enumerate(
                (
                    (mine_ref.at[same, :, j], pair_ref.at[j, m]),
                    (mine_ref.at[cross, :, j], key_ref.at[j, cross]),
                    (other_ref.at[same, :, j], key_ref.at[j, same]),
                )
            ):
                loads.append(pltpu.make_async_copy(source, target, sem.at[k]))
    for load in loads:
        load.start()
    key_acc[...] = jnp.zeros_like(key_acc)
    value_acc[...] = jnp.zeros_like(value_acc)
    for load in loads:
        load.wait()

    def work(j, m, span):
        i = 2 * m + core
        low = i - (span - 1)
        width = span * block
        query = pair_ref[j, m, :, 0].reshape(block, HEAD_DIM)
        cot = pair_ref[j, m, :, 1].reshape(block, HEAD_DIM)
        key = key_ref[j, pl.ds(low, span), :, 0].reshape(width, HEAD_DIM)
        value = key_ref[j, pl.ds(low, span), :, 1].reshape(width, HEAD_DIM)
        start = start_ref[pl.ds(pl.multiple_of(i * block, block), block), :] - low * block
        col = lax.broadcasted_iota(jnp.int32, (block, width), 1)
        row = lax.broadcasted_iota(jnp.int32, (block, width), 0) + (span - 1) * block
        allowed = (col >= start) & (col <= row)
        score = jnp.where(allowed, dot_nt(query, key), NEG)
        peak = jnp.max(score, axis=1, keepdims=True)
        expo = jnp.exp2((score - peak) * EXP_SCALE)
        inverse = 1.0 / jnp.sum(expo, axis=1, keepdims=True)
        weight = expo * inverse
        weight_low = weight.astype(jnp.bfloat16)
        mixed = dot_nn(weight_low, value)
        rowdot = jnp.sum(mixed * cot.astype(jnp.float32), axis=1, keepdims=True)
        dscore = (weight * (dot_nt(cot, value) - rowdot)).astype(jnp.bfloat16)
        mixed_ref[m, j, 0] = mixed.astype(jnp.bfloat16)
        mixed_ref[m, j, 1] = (SCALE * dot_nn(dscore, key)).astype(jnp.bfloat16)
        held = pl.ds(pl.multiple_of(low * block, block), width)
        key_acc[j, held, :] += dot_tn(dscore, query)
        value_acc[j, held, :] += dot_tn(weight_low, cot)

    def step(n, carry):
        j, m = n // group, n % group
        for span in range(1, spans + 1):
            pl.when(count_ref[2 * m + core] == span)(functools.partial(work, j, m, span))
        return carry

    lax.fori_loop(0, size * group, step, 0)
    moves = [
        pltpu.make_async_copy(mixed_ref.at[place_ref[1 + d]], outs[d], sems.at[d])
        for d in range(group)
    ]
    for move in moves:
        move.start()

    def finish(n, carry):
        j, m = n // group, n % group
        own = pl.ds(pl.multiple_of((2 * m + core) * block, block), block)
        cross = pl.ds(pl.multiple_of((2 * m + 1 - core) * block, block), block)
        keep_ref[m, j, 0] = SCALE * key_acc[j, own, :]
        keep_ref[m, j, 1] = value_acc[j, own, :]
        send_ref[m, j, 0] = (SCALE * key_acc[j, cross, :]).astype(jnp.bfloat16)
        send_ref[m, j, 1] = value_acc[j, cross, :].astype(jnp.bfloat16)
        return carry

    lax.fori_loop(0, size * group, finish, 0)
    for move in moves:
        move.wait()


def attention(count, place, start, mine, other):
    shards, chans, size, _, rows, _ = mine.shape
    group = shards // 2
    block = chans * rows
    total = shards * block
    spans = min(shards, (DOC_MAX + block - 2) // block + 1)
    pairs = size * group * block * block * min(spans, 3)
    return pl.pallas_call(
        functools.partial(attention_kernel, spans, size, group),
        out_shape=[low_array(size, 2, block, HEAD_DIM)] * group
        + [
            jax.ShapeDtypeStruct((group, size, 2, block, HEAD_DIM), jnp.float32),
            low_array(group, size, 2, block, HEAD_DIM),
        ],
        in_specs=[SCALARS, SCALARS, VECTORS, ANYWHERE, ANYWHERE],
        out_specs=[ANYWHERE] * group + [VECTORS] * 2,
        scratch_shapes=[
            pltpu.VMEM((size, group, chans, 2, rows, HEAD_DIM), jnp.bfloat16),
            pltpu.VMEM((size, shards, chans, 2, rows, HEAD_DIM), jnp.bfloat16),
            pltpu.VMEM((group, size, 2, block, HEAD_DIM), jnp.bfloat16),
            pltpu.VMEM((size, total, HEAD_DIM), jnp.float32),
            pltpu.VMEM((size, total, HEAD_DIM), jnp.float32),
            pltpu.SemaphoreType.DMA((size, group, 3)),
            pltpu.SemaphoreType.DMA((group,)),
        ],
        compiler_params=pltpu.CompilerParams(vmem_limit_bytes=48 * 1024 * 1024),
        cost_estimate=pl.CostEstimate(
            flops=12 * HEAD_DIM * pairs,
            bytes_accessed=10 * size * total * HEAD_DIM,
            transcendentals=pairs,
        ),
    )(count, place, start, mine, other)


def add_kernel(place_ref, keep_ref, other_ref, *outs):
    for d, out_ref in enumerate(outs):
        m = place_ref[1 + d]
        out_ref[...] = (keep_ref[m] + other_ref[m].astype(jnp.float32)).astype(jnp.bfloat16)


def add(place, keep, other):
    group = keep.shape[0]
    return pl.pallas_call(
        add_kernel,
        out_shape=[low_array(*keep.shape[1:])] * group,
        in_specs=[SCALARS, VECTORS, VECTORS],
        out_specs=[VECTORS] * group,
        compiler_params=pltpu.CompilerParams(vmem_limit_bytes=32 * 1024 * 1024),
        cost_estimate=moved(8 * keep.size),
    )(place, keep, other)


def unpack_kernel(group, size, place_ref, *refs):
    mixed, grads, outs = refs[:group], refs[group : 2 * group], refs[-4:]
    for d in range(group):
        for j in range(size):
            head = place_ref[1 + d] * size + j
            columns = pl.ds(pl.multiple_of(head * HEAD_DIM, HEAD_DIM), HEAD_DIM)
            for which in range(2):
                outs[which][:, columns] = mixed[d][j, which]
                outs[2 + which][:, columns] = grads[d][j, which]


def unpack(place, mixed, grads, width, offset, held):
    group = len(mixed)
    size, _, rows, _ = mixed[0].shape
    step = min(rows, 64)
    return pl.pallas_call(
        functools.partial(unpack_kernel, group, size),
        grid=(rows // step,),
        out_shape=[low_array(rows, width)] * 4,
        in_specs=[SCALARS]
        + [pl.BlockSpec((size, 2, step, HEAD_DIM), lambda i: (0, 0, i, 0))] * (2 * group)
        + [ANYWHERE] * len(held),
        out_specs=[pl.BlockSpec((step, group * size * HEAD_DIM), lambda i: (i, offset // size))] * 4,
        input_output_aliases={1 + 2 * group + i: i for i in range(len(held))},
        cost_estimate=moved(16 * group * size * rows * HEAD_DIM),
    )(place, *mixed, *grads, *held)


def exchange(value, d):
    return lax.ppermute(value, "seq", [(s, s ^ d) for s in range(lax.axis_size("seq"))])


def on_device(doc_ids, *inputs):
    shards = lax.axis_size("seq")
    chans = lax.axis_size("chan")
    rows, width = inputs[0].shape
    heads = width // HEAD_DIM // chans
    group = shards // 2
    block = rows * chans
    start = jnp.sum((doc_ids[None, :] < doc_ids[:, None]).astype(jnp.int32), axis=1)
    count = jnp.arange(shards, dtype=jnp.int32) - start[::block] // block + 1
    start = start[:, None]
    shard = lax.axis_index("seq")
    chips = jnp.bitwise_xor(shard // 2, jnp.arange(group, dtype=jnp.int32))
    place = jnp.concatenate([(shard % 2)[None].astype(jnp.int32), chips])

    gathered = []
    for chunk in range(heads // group):
        parts = pack(place, inputs, chans, group, chunk, 1)
        parts = parts.reshape(shards * chans, 1, 2, rows, HEAD_DIM)
        mine = lax.all_to_all(parts, ("seq", "chan"), split_axis=0, concat_axis=0, tiled=True)
        gathered.append(mine.reshape(shards, chans, 1, 2, rows, HEAD_DIM))

    outs, sent = (), ()
    for chunk, mine in enumerate(gathered):
        mine, outs, sent = lax.optimization_barrier((mine, outs, sent))
        if chunk > 0:
            outs = unpack(place, *sent, heads * HEAD_DIM, chunk - 1, outs)
        *mixed, keep, send = attention(count, place, start, mine, exchange(mine, 1))
        mixed = [mixed[0]] + [exchange(mixed[d], 2 * d) for d in range(1, group)]
        grads = add(place, keep, exchange(send, 1))
        grads = [grads[0]] + [exchange(grads[d], 2 * d) for d in range(1, group)]
        sent = (mixed, grads)
    return tuple(unpack(place, *sent, heads * HEAD_DIM, len(gathered) - 1, outs))


def solution(mesh):
    spread = P(("seq", "chan"), None)
    in_specs = (P(), spread, spread, spread, spread)
    out_specs = (P("seq", "chan"),) * 4
    return jax.shard_map(
        on_device, mesh=mesh, in_specs=in_specs, out_specs=out_specs, check_vma=False
    )
```

profile of v0, /device:TPU:9, one launch (start us, length us, event | category | flops | bytes accessed | tf_op | source)
XLA Modules:
  0.0 203.2 jit_solution(3807227056420893900)
XLA Ops:
  1.2 3.4 %shard_map.87 = bf16[8,4,1,2,64,128]{5,4,3,2,1,0:T(8,128)(2,1)} custom-call(s32[5]{0:T(128)} %pad_add_fusion.place_ref.refs_1_, bf16[64,8192]{1,0:T(8,128)(2,1)} %refs_0_.7, bf16[64,8192]{1,0:T(8,128)(2,1)} %refs_1_.7, bf16[64,8192]{1,0:T(8,128)(2,1)} %refs_2_.7, bf16[64,8192]{1,0:T(8,128)(2,1)} %refs_3_.7), custom_call_target="tpu_custom_call" | custom-call | bytes 2097152 | tf_op jit(solution)/shard_map/pallas_call | solution.py:57
  4.6 6.4 %all-to-all-start.3 = ((bf16[32,1,2,64,128]{4,3,2,1,0:T(8,128)(2,1)}), bf16[32,1,2,64,128]{4,3,2,1,0:T(8,128)(2,1)S(1)}, u32[]{:S(2)}, u32[]{:S(2)}) async-start(bf16[32,1,2,64,128]{4,3,2,1,0:T(8,128)(2,1)} %bitcast.29), calls=%async_computation.3 | async-start | bytes 2097152 | tf_op jit(solution)/shard_map/all_to_all | solution.py:254
  11.0 3.4 %shard_map.86 = bf16[8,4,1,2,64,128]{5,4,3,2,1,0:T(8,128)(2,1)} custom-call(s32[5]{0:T(128)} %pad_add_fusion.place_ref.refs_1_, bf16[64,8192]{1,0:T(8,128)(2,1)} %refs_0_.7, bf16[64,8192]{1,0:T(8,128)(2,1)} %refs_1_.7, bf16[64,8192]{1,0:T(8,128)(2,1)} %refs_2_.7, bf16[64,8192]{1,0:T(8,128)(2,1)} %refs_3_.7), custom_call_target="tpu_custom_call" | custom-call | bytes 2097152 | tf_op jit(solution)/shard_map/pallas_call | solution.py:57
  14.5 21.3 %all-to-all-done.3 = bf16[32,1,2,64,128]{4,3,2,1,0:T(8,128)(2,1)S(1)} async-done(((bf16[32,1,2,64,128]{4,3,2,1,0:T(8,128)(2,1)}), bf16[32,1,2,64,128]{4,3,2,1,0:T(8,128)(2,1)S(1)}, u32[]{:S(2)}, u32[]{:S(2)}) %all-to-all-start.3) | async-done | bytes 1048608 | tf_op jit(solution)/shard_map/all_to_all | solution.py:254
  35.7 4.8 %all-to-all-start.2 = ((bf16[32,1,2,64,128]{4,3,2,1,0:T(8,128)(2,1)}), bf16[32,1,2,64,128]{4,3,2,1,0:T(8,128)(2,1)S(1)}, u32[]{:S(2)}, u32[]{:S(2)}) async-start(bf16[32,1,2,64,128]{4,3,2,1,0:T(8,128)(2,1)} %bitcast.28), calls=%async_computation.2 | async-start | bytes 2097152 | tf_op jit(solution)/shard_map/all_to_all | solution.py:254
  43.4 9.6 %shard_map.88 = (bf16[1,2,256,128]{3,2,1,0:T(8,128)(2,1)S(1)}, bf16[1,2,256,128]{3,2,1,0:T(8,128)(2,1)S(1)}, bf16[1,2,256,128]{3,2,1,0:T(8,128)(2,1)S(1)}, bf16[...) custom-call(s32[8]{0:T(128)S(1)} %subtract_add_fusion.refs_0_, ...), custom_call_target="tpu_custom_call" | custom-call | flops 1207959552 | bytes 2621440 | tf_op jit(solution)/shard_map/pallas_call | solution.py:159
  54.7 3.4 %shard_map.85 = bf16[8,4,1,2,64,128]{5,4,3,2,1,0:T(8,128)(2,1)} custom-call(s32[5]{0:T(128)} %pad_add_fusion.place_ref.refs_1_, bf16[64,8192]{1,0:T(8,128)(2,1)} %refs_0_.7, bf16[64,8192]{1,0:T(8,128)(2,1)} %refs_1_.7, bf16[64,8192]{1,0:T(8,128)(2,1)} %refs_2_.7, bf16[64,8192]{1,0:T(8,128)(2,1)} %refs_3_.7), custom_call_target="tpu_custom_call" | custom-call | bytes 2097152 | tf_op jit(solution)/shard_map/pallas_call | solution.py:57
  58.1 7.1 %all-to-all-done.2 = bf16[32,1,2,64,128]{4,3,2,1,0:T(8,128)(2,1)S(1)} async-done(((bf16[32,1,2,64,128]{4,3,2,1,0:T(8,128)(2,1)}), bf16[32,1,2,64,128]{4,3,2,1,0:T(8,128)(2,1)S(1)}, u32[]{:S(2)}, u32[]{:S(2)}) %all-to-all-start.2) | async-done | bytes 1048608 | tf_op jit(solution)/shard_map/all_to_all | solution.py:254
  65.2 4.8 %all-to-all-start.1 = ((bf16[32,1,2,64,128]{4,3,2,1,0:T(8,128)(2,1)}), bf16[32,1,2,64,128]{4,3,2,1,0:T(8,128)(2,1)S(1)}, u32[]{:S(2)}, u32[]{:S(2)}) async-start(bf16[32,1,2,64,128]{4,3,2,1,0:T(8,128)(2,1)} %bitcast.27), calls=%async_computation.1 | async-start | bytes 2097152 | tf_op jit(solution)/shard_map/all_to_all | solution.py:254
  78.2 3.4 %collective-permute-done.1.refs_1_ = bf16[1,2,256,128]{3,2,1,0:T(8,128)(2,1)S(1)} collective-permute-done((bf16[1,2,256,128]{3,2,1,0:T(8,128)(2,1)S(1)}, bf16[1,2,256,128]{3,2,1,0:T(8,128)(2,1)S(1)}, u32[]{:S(2)}, u32[]{:S(2)}) %collective-permute-start.1) | collective-permute-done | bytes 131104 | tf_op jit(solution)/shard_map/ppermute | solution.py:233
  82.8 4.2 %collective-permute-done.3.refs_3_ = bf16[1,2,256,128]{3,2,1,0:T(8,128)(2,1)S(1)} collective-permute-done((bf16[1,2,256,128]{3,2,1,0:T(8,128)(2,1)S(1)}, bf16[1,2,256,128]{3,2,1,0:T(8,128)(2,1)S(1)}, u32[]{:S(2)}, u32[]{:S(2)}) %collective-permute-start.3) | collective-permute-done | bytes 131104 | tf_op jit(solution)/shard_map/ppermute | solution.py:233
  87.0 3.8 %collective-permute-done.5.refs_5_ = bf16[1,2,256,128]{3,2,1,0:T(8,128)(2,1)S(1)} collective-permute-done((bf16[1,2,256,128]{3,2,1,0:T(8,128)(2,1)S(1)}, bf16[1,2,256,128]{3,2,1,0:T(8,128)(2,1)S(1)}, u32[]{:S(2)}, u32[]{:S(2)}) %collective-permute-start.5) | collective-permute-done | bytes 131104 | tf_op jit(solution)/shard_map/ppermute | solution.py:233
  90.9 4.3 %collective-permute-done.7.refs_7_ = bf16[1,2,256,128]{3,2,1,0:T(8,128)(2,1)S(1)} collective-permute-done((bf16[1,2,256,128]{3,2,1,0:T(8,128)(2,1)S(1)}, bf16[1,2,256,128]{3,2,1,0:T(8,128)(2,1)S(1)}, u32[]{:S(2)}, u32[]{:S(2)}) %collective-permute-start.7) | collective-permute-done | bytes 131104 | tf_op jit(solution)/shard_map/ppermute | solution.py:233
  96.1 2.3 %collective-permute-done.8.refs_4_ = bf16[8,4,1,2,64,128]{5,4,3,2,1,0:T(8,128)(2,1)S(1)} collective-permute-done((bf16[8,4,1,2,64,128]{5,4,3,2,1,0:T(8,128)(2,1)S(1)}, bf16[8,4,1,2,64,128]{5,4,3,2,1,0:T(8,128)(2,1)S(1)}, u32[]{:S(2)}, u32[]{:S(2)}) %collective-permute-start.8) | collective-permute-done | bytes 1048608 | tf_op jit(solution)/shard_map/ppermute | solution.py:233
  98.4 9.6 %shard_map.91 = (bf16[1,2,256,128]{3,2,1,0:T(8,128)(2,1)S(1)}, bf16[1,2,256,128]{3,2,1,0:T(8,128)(2,1)S(1)}, bf16[1,2,256,128]{3,2,1,0:T(8,128)(2,1)S(1)}, bf16[...) custom-call(s32[8]{0:T(128)S(1)} %subtract_add_fusion.refs_0_, ...), custom_call_target="tpu_custom_call" | custom-call | flops 1207959552 | bytes 2621440 | tf_op jit(solution)/shard_map/pallas_call | solution.py:159
  109.9 3.4 %shard_map.84 = bf16[8,4,1,2,64,128]{5,4,3,2,1,0:T(8,128)(2,1)} custom-call(s32[5]{0:T(128)} %pad_add_fusion.place_ref.refs_1_, bf16[64,8192]{1,0:T(8,128)(2,1)} %refs_0_.7, bf16[64,8192]{1,0:T(8,128)(2,1)} %refs_1_.7, bf16[64,8192]{1,0:T(8,128)(2,1)} %refs_2_.7, bf16[64,8192]{1,0:T(8,128)(2,1)} %refs_3_.7), custom_call_target="tpu_custom_call" | custom-call | bytes 2097152 | tf_op jit(solution)/shard_map/pallas_call | solution.py:57
  113.3 6.4 %all-to-all-start = ((bf16[32,1,2,64,128]{4,3,2,1,0:T(8,128)(2,1)}), bf16[32,1,2,64,128]{4,3,2,1,0:T(8,128)(2,1)S(1)}, u32[]{:S(2)}, u32[]{:S(2)}) async-start(bf16[32,1,2,64,128]{4,3,2,1,0:T(8,128)(2,1)} %bitcast.26), calls=%async_computation | async-start | bytes 2097152 | tf_op jit(solution)/shard_map/all_to_all | solution.py:254
  119.8 2.1 %collective-permute-start.11 = (bf16[1,2,256,128]{3,2,1,0:T(8,128)(2,1)S(1)}, bf16[1,2,256,128]{3,2,1,0:T(8,128)(2,1)}, u32[]{:S(2)}, u32[]{:S(2)}) collective-permute-start(bf16[1,2,256,128]{3,2,1,0:T(8,128)(2,1)S(1)} %get-tuple-element.117), channel_id=1, source_target_pairs={{0,24},{4,28},{8,16},{12,20},{16,8},{20,12},{24,0},{28,4},{1,25},{... | collective-permute-start | bytes 393224 | tf_op jit(solution)/shard_map/ppermute | solution.py:233
  128.6 3.3 %shard_map.90 = (bf16[256,2048]{1,0:T(8,128)(2,1)}, bf16[256,2048]{1,0:T(8,128)(2,1)}, bf16[256,2048]{1,0:T(8,128)(2,1)}, bf16[256,2048]{1,0:T(8,128)(2,1)}) custom-call(s32[5]{0:T(128)} %pad_add_fusion.place_ref.refs_1_, bf16[1,2,256,128]{3,2,1,0:T(8,128)(2,1)} %copy-done.10, bf16[1,2,256,128]{3,2,1,0:T(8,128)(2,1)} %copy-done.28, ...), custom_call_target="tpu_custom_call" | custom-call | bytes 2097152 | tf_op jit(solution)/shard_map/pallas_call | solution.py:219
  133.1 4.8 %collective-permute-done.9.refs_1_ = bf16[1,2,256,128]{3,2,1,0:T(8,128)(2,1)} collective-permute-done((bf16[1,2,256,128]{3,2,1,0:T(8,128)(2,1)S(1)}, bf16[1,2,256,128]{3,2,1,0:T(8,128)(2,1)}, u32[]{:S(2)}, u32[]{:S(2)}) %collective-permute-start.9) | collective-permute-done | bytes 131104 | tf_op jit(solution)/shard_map/ppermute | solution.py:233
  137.9 3.5 %collective-permute-done.13.refs_5_ = bf16[1,2,256,128]{3,2,1,0:T(8,128)(2,1)} collective-permute-done((bf16[1,2,256,128]{3,2,1,0:T(8,128)(2,1)}, bf16[1,2,256,128]{3,2,1,0:T(8,128)(2,1)}, u32[]{:S(2)}, u32[]{:S(2)}) %collective-permute-start.13) | collective-permute-done | bytes 131104 | tf_op jit(solution)/shard_map/ppermute | solution.py:233
  141.4 4.6 %collective-permute-done.15.refs_7_ = bf16[1,2,256,128]{3,2,1,0:T(8,128)(2,1)S(1)} collective-permute-done((bf16[1,2,256,128]{3,2,1,0:T(8,128)(2,1)}, bf16[1,2,256,128]{3,2,1,0:T(8,128)(2,1)S(1)}, u32[]{:S(2)}, u32[]{:S(2)}) %collective-permute-start.15) | collective-permute-done | bytes 131104 | tf_op jit(solution)/shard_map/ppermute | solution.py:233
  146.9 2.3 %collective-permute-done.16.refs_4_ = bf16[8,4,1,2,64,128]{5,4,3,2,1,0:T(8,128)(2,1)S(1)} collective-permute-done((bf16[8,4,1,2,64,128]{5,4,3,2,1,0:T(8,128)(2,1)S(1)}, bf16[8,4,1,2,64,128]{5,4,3,2,1,0:T(8,128)(2,1)S(1)}, u32[]{:S(2)}, u32[]{:S(2)}) %collective-permute-start.16) | collective-permute-done | bytes 1048608 | tf_op jit(solution)/shard_map/ppermute | solution.py:233
  149.2 8.8 %shard_map.94 = (bf16[1,2,256,128]{3,2,1,0:T(8,128)(2,1)S(1)}, bf16[1,2,256,128]{3,2,1,0:T(8,128)(2,1)S(1)}, bf16[1,2,256,128]{3,2,1,0:T(8,128)(2,1)S(1)}, bf16[...) custom-call(s32[8]{0:T(128)S(1)} %subtract_add_fusion.refs_0_, ...), custom_call_target="tpu_custom_call" | custom-call | flops 1207959552 | bytes 2621440 | tf_op jit(solution)/shard_map/pallas_call | solution.py:159
  158.9 2.0 collective-permute-start.19
  162.9 1.9 collective-permute-start.23
  164.8 3.3 %shard_map.93 = (bf16[256,2048]{1,0:T(8,128)(2,1)}, bf16[256,2048]{1,0:T(8,128)(2,1)}, bf16[256,2048]{1,0:T(8,128)(2,1)}, bf16[256,2048]{1,0:T(8,128)(2,1)}) custom-call(s32[5]{0:T(128)} %pad_add_fusion.place_ref.refs_1_, bf16[1,2,256,128]{3,2,1,0:T(8,128)(2,1)} %copy-done.4, ...), custom_call_target="tpu_custom_call", output_to_operand_aliasing={{0}: (9, {}), {1}: (10, {}), {2}: (11, {}), {3}: (12, {})} | custom-call | bytes 2097152 | tf_op jit(solution)/shard_map/pallas_call | solution.py:219
  172.9 2.3 %collective-permute-done.24.refs_4_ = bf16[8,4,1,2,64,128]{5,4,3,2,1,0:T(8,128)(2,1)S(1)} collective-permute-done((bf16[8,4,1,2,64,128]{5,4,3,2,1,0:T(8,128)(2,1)S(1)}, bf16[8,4,1,2,64,128]{5,4,3,2,1,0:T(8,128)(2,1)S(1)}, u32[]{:S(2)}, u32[]{:S(2)}) %collective-permute-start.24) | collective-permute-done | bytes 1048608 | tf_op jit(solution)/shard_map/ppermute | solution.py:233
  175.2 9.0 %shard_map.96 = (bf16[1,2,256,128]{3,2,1,0:T(8,128)(2,1)S(1)}, bf16[1,2,256,128]{3,2,1,0:T(8,128)(2,1)S(1)}, bf16[1,2,256,128]{3,2,1,0:T(8,128)(2,1)S(1)}, bf16[...) custom-call(s32[8]{0:T(128)S(1)} %subtract_add_fusion.refs_0_, ...), custom_call_target="tpu_custom_call" | custom-call | flops 1207959552 | bytes 2621440 | tf_op jit(solution)/shard_map/pallas_call | solution.py:159
  191.0 3.3 %shard_map.98 = (bf16[256,2048]{1,0:T(8,128)(2,1)}, bf16[256,2048]{1,0:T(8,128)(2,1)}, bf16[256,2048]{1,0:T(8,128)(2,1)}, bf16[256,2048]{1,0:T(8,128)(2,1)}) custom-call(s32[5]{0:T(128)} %pad_add_fusion.place_ref.refs_1_, bf16[1,2,256,128]{3,2,1,0:T(8,128)(2,1)} %copy-done.5, ...), custom_call_target="tpu_custom_call", output_to_operand_aliasing={{0}: (9, {}), {1}: (10, {}), {2}: (11, {}), {3}: (12, {})} | custom-call | bytes 2097152 | tf_op jit(solution)/shard_map/pallas_call | solution.py:219
  194.5 4.5 %collective-permute-done.30.refs_6_ = bf16[1,2,256,128]{3,2,1,0:T(8,128)(2,1)S(1)} collective-permute-done((bf16[1,2,256,128]{3,2,1,0:T(8,128)(2,1)S(1)}, bf16[1,2,256,128]{3,2,1,0:T(8,128)(2,1)S(1)}, u32[]{:S(2)}, u32[]{:S(2)}) %collective-permute-start.30) | collective-permute-done | bytes 131104 | tf_op jit(solution)/shard_map/ppermute | solution.py:233
  199.8 3.3 %shard_map.99 = (bf16[256,2048]{1,0:T(8,128)(2,1)}, bf16[256,2048]{1,0:T(8,128)(2,1)}, bf16[256,2048]{1,0:T(8,128)(2,1)}, bf16[256,2048]{1,0:T(8,128)(2,1)}) custom-call(s32[5]{0:T(128)} %pad_add_fusion.place_ref.refs_1_, bf16[1,2,256,128]{3,2,1,0:T(8,128)(2,1)} %copy-done.8, ...), custom_call_target="tpu_custom_call", output_to_operand_aliasing={{0}: (9, {}), {1}: (10, {}), {2}: (11, {}), {3}: (12, {})} | custom-call | bytes 2097152 | tf_op jit(solution)/shard_map/pallas_call | solution.py:219
  (132 shorter events, 41.3 us)
Async XLA Ops:
  4.6 31.1 %all-to-all-start.3 = ((bf16[32,1,2,64,128]{4,3,2,1,0:T(8,128)(2,1)}), bf16[32,1,2,64,128]{4,3,2,1,0:T(8,128)(2,1)S(1)}, u32[]{:S(2)}, u32[]{:S(2)}) async-start(bf16[32,1,2,64,128]{4,3,2,1,0:T(8,128)(2,1)} %bitcast.29), calls=%async_computation.3 | async-start | bytes 2097152 | tf_op jit(solution)/shard_map/all_to_all | solution.py:254
  35.7 29.5 %all-to-all-start.2 = ((bf16[32,1,2,64,128]{4,3,2,1,0:T(8,128)(2,1)}), bf16[32,1,2,64,128]{4,3,2,1,0:T(8,128)(2,1)S(1)}, u32[]{:S(2)}, u32[]{:S(2)}) async-start(bf16[32,1,2,64,128]{4,3,2,1,0:T(8,128)(2,1)} %bitcast.28), calls=%async_computation.2 | async-start | bytes 2097152 | tf_op jit(solution)/shard_map/all_to_all | solution.py:254
  54.7 18.1 %collective-permute-start.4 = (bf16[4,1,2,256,128]{4,3,2,1,0:T(8,128)(2,1)}, bf16[4,1,2,256,128]{4,3,2,1,0:T(8,128)(2,1)}, u32[]{:S(2)}, u32[]{:S(2)}) collective-permute-start(bf16[4,1,2,256,128]{4,3,2,1,0:T(8,128)(2,1)} %get-tuple-element.96), channel_id=1, source_target_pairs={{0,4},{4,0},{8,12},{12,8},{16,20},{20,16},{24,28},{28,24},{1,5},{5... | collective-permute-start | bytes 1572872 | tf_op jit(solution)/shard_map/ppermute | solution.py:233
  65.2 48.1 %all-to-all-start.1 = ((bf16[32,1,2,64,128]{4,3,2,1,0:T(8,128)(2,1)}), bf16[32,1,2,64,128]{4,3,2,1,0:T(8,128)(2,1)S(1)}, u32[]{:S(2)}, u32[]{:S(2)}) async-start(bf16[32,1,2,64,128]{4,3,2,1,0:T(8,128)(2,1)} %bitcast.27), calls=%async_computation.1 | async-start | bytes 2097152 | tf_op jit(solution)/shard_map/all_to_all | solution.py:254
  70.1 11.5 %collective-permute-start.1 = (bf16[1,2,256,128]{3,2,1,0:T(8,128)(2,1)S(1)}, bf16[1,2,256,128]{3,2,1,0:T(8,128)(2,1)S(1)}, u32[]{:S(2)}, u32[]{:S(2)}) collective-permute-start(bf16[1,2,256,128]{3,2,1,0:T(8,128)(2,1)S(1)} %get-tuple-element.92), channel_id=1, source_target_pairs={{0,8},{4,12},{8,0},{12,4},{16,24},{20,28},{24,16},{28,20},{1,9},{5... | collective-permute-start | bytes 393224 | tf_op jit(solution)/shard_map/ppermute | solution.py:233
  71.3 11.5 %collective-permute-start.2 = (bf16[1,2,256,128]{3,2,1,0:T(8,128)(2,1)S(1)}, bf16[1,2,256,128]{3,2,1,0:T(8,128)(2,1)S(1)}, u32[]{:S(2)}, u32[]{:S(2)}) collective-permute-start(bf16[1,2,256,128]{3,2,1,0:T(8,128)(2,1)S(1)} %get-tuple-element.93), channel_id=1, source_target_pairs={{0,16},{4,20},{8,24},{12,28},{16,0},{20,4},{24,8},{28,12},{1,17},{... | collective-permute-start | bytes 393224 | tf_op jit(solution)/shard_map/ppermute | solution.py:233
  72.5 14.5 %collective-permute-start.3 = (bf16[1,2,256,128]{3,2,1,0:T(8,128)(2,1)S(1)}, bf16[1,2,256,128]{3,2,1,0:T(8,128)(2,1)S(1)}, u32[]{:S(2)}, u32[]{:S(2)}) collective-permute-start(bf16[1,2,256,128]{3,2,1,0:T(8,128)(2,1)S(1)} %get-tuple-element.94), channel_id=1, source_target_pairs={{0,24},{4,28},{8,16},{12,20},{16,8},{20,12},{24,0},{28,4},{1,25},{... | collective-permute-start | bytes 393224 | tf_op jit(solution)/shard_map/ppermute | solution.py:233
  75.8 15.0 %collective-permute-start.5 = (bf16[1,2,256,128]{3,2,1,0:T(8,128)(2,1)S(1)}, bf16[1,2,256,128]{3,2,1,0:T(8,128)(2,1)S(1)}, u32[]{:S(2)}, u32[]{:S(2)}) collective-permute-start(bf16[1,2,256,128]{3,2,1,0:T(8,128)(2,1)S(1)} %get-tuple-element.98), channel_id=1, source_target_pairs={{0,8},{4,12},{8,0},{12,4},{16,24},{20,28},{24,16},{28,20},{1,9},{5... | collective-permute-start | bytes 393224 | tf_op jit(solution)/shard_map/ppermute | solution.py:233
  77.0 13.9 %collective-permute-start.6 = (bf16[1,2,256,128]{3,2,1,0:T(8,128)(2,1)S(1)}, bf16[1,2,256,128]{3,2,1,0:T(8,128)(2,1)S(1)}, u32[]{:S(2)}, u32[]{:S(2)}) collective-permute-start(bf16[1,2,256,128]{3,2,1,0:T(8,128)(2,1)S(1)} %get-tuple-element.99), channel_id=1, source_target_pairs={{0,16},{4,20},{8,24},{12,28},{16,0},{20,4},{24,8},{28,12},{1,17},{... | collective-permute-start | bytes 393224 | tf_op jit(solution)/shard_map/ppermute | solution.py:233
  81.6 13.6 %collective-permute-start.7 = (bf16[1,2,256,128]{3,2,1,0:T(8,128)(2,1)S(1)}, bf16[1,2,256,128]{3,2,1,0:T(8,128)(2,1)S(1)}, u32[]{:S(2)}, u32[]{:S(2)}) collective-permute-start(bf16[1,2,256,128]{3,2,1,0:T(8,128)(2,1)S(1)} %get-tuple-element.100), channel_id=1, source_target_pairs={{0,24},{4,28},{8,16},{12,20},{16,8},{20,12},{24,0},{28,4},{1,25},{... | collective-permute-start | bytes 393224 | tf_op jit(solution)/shard_map/ppermute | solution.py:233
  109.6 12.6 %collective-permute-start.12 = (bf16[4,1,2,256,128]{4,3,2,1,0:T(8,128)(2,1)}, bf16[4,1,2,256,128]{4,3,2,1,0:T(8,128)(2,1)}, u32[]{:S(2)}, u32[]{:S(2)}) collective-permute-start(bf16[4,1,2,256,128]{4,3,2,1,0:T(8,128)(2,1)} %get-tuple-element.119), channel_id=1, source_target_pairs={{0,4},{4,0},{8,12},{12,8},{16,20},{20,16},{24,28},{28,24},{1,5},{5... | collective-permute-start | bytes 1572872 | tf_op jit(solution)/shard_map/ppermute | solution.py:233
  109.6 17.8 %collective-permute-start.10 = (bf16[1,2,256,128]{3,2,1,0:T(8,128)(2,1)S(1)}, bf16[1,2,256,128]{3,2,1,0:T(8,128)(2,1)}, u32[]{:S(2)}, u32[]{:S(2)}) collective-permute-start(bf16[1,2,256,128]{3,2,1,0:T(8,128)(2,1)S(1)} %get-tuple-element.116), channel_id=1, source_target_pairs={{0,16},{4,20},{8,24},{12,28},{16,0},{20,4},{24,8},{28,12},{1,17},{... | collective-permute-start | bytes 393224 | tf_op jit(solution)/shard_map/ppermute | solution.py:233
  113.3 54.8 %all-to-all-start = ((bf16[32,1,2,64,128]{4,3,2,1,0:T(8,128)(2,1)}), bf16[32,1,2,64,128]{4,3,2,1,0:T(8,128)(2,1)S(1)}, u32[]{:S(2)}, u32[]{:S(2)}) async-start(bf16[32,1,2,64,128]{4,3,2,1,0:T(8,128)(2,1)} %bitcast.26), calls=%async_computation | async-start | bytes 2097152 | tf_op jit(solution)/shard_map/all_to_all | solution.py:254
  119.8 13.4 %collective-permute-start.11 = (bf16[1,2,256,128]{3,2,1,0:T(8,128)(2,1)S(1)}, bf16[1,2,256,128]{3,2,1,0:T(8,128)(2,1)}, u32[]{:S(2)}, u32[]{:S(2)}) collective-permute-start(bf16[1,2,256,128]{3,2,1,0:T(8,128)(2,1)S(1)} %get-tuple-element.117), channel_id=1, source_target_pairs={{0,24},{4,28},{8,16},{12,20},{16,8},{20,12},{24,0},{28,4},{1,25},{... | collective-permute-start | bytes 393224 | tf_op jit(solution)/shard_map/ppermute | solution.py:233
  121.9 16.0 %collective-permute-start.9 = (bf16[1,2,256,128]{3,2,1,0:T(8,128)(2,1)S(1)}, bf16[1,2,256,128]{3,2,1,0:T(8,128)(2,1)}, u32[]{:S(2)}, u32[]{:S(2)}) collective-permute-start(bf16[1,2,256,128]{3,2,1,0:T(8,128)(2,1)S(1)} %get-tuple-element.115), channel_id=1, source_target_pairs={{0,8},{4,12},{8,0},{12,4},{16,24},{20,28},{24,16},{28,20},{1,9},{5... | collective-permute-start | bytes 393224 | tf_op jit(solution)/shard_map/ppermute | solution.py:233
  125.9 15.5 %collective-permute-start.13 = (bf16[1,2,256,128]{3,2,1,0:T(8,128)(2,1)}, bf16[1,2,256,128]{3,2,1,0:T(8,128)(2,1)}, u32[]{:S(2)}, u32[]{:S(2)}) collective-permute-start(bf16[1,2,256,128]{3,2,1,0:T(8,128)(2,1)} %get-tuple-element.121), channel_id=1, source_target_pairs={{0,8},{4,12},{8,0},{12,4},{16,24},{20,28},{24,16},{28,20},{1,9},{5... | collective-permute-start | bytes 393224 | tf_op jit(solution)/shard_map/ppermute | solution.py:233
  127.1 14.3 %collective-permute-start.14 = (bf16[1,2,256,128]{3,2,1,0:T(8,128)(2,1)}, bf16[1,2,256,128]{3,2,1,0:T(8,128)(2,1)}, u32[]{:S(2)}, u32[]{:S(2)}) collective-permute-start(bf16[1,2,256,128]{3,2,1,0:T(8,128)(2,1)} %get-tuple-element.122), channel_id=1, source_target_pairs={{0,16},{4,20},{8,24},{12,28},{16,0},{20,4},{24,8},{28,12},{1,17},{... | collective-permute-start | bytes 393224 | tf_op jit(solution)/shard_map/ppermute | solution.py:233
  127.4 18.6 %collective-permute-start.15 = (bf16[1,2,256,128]{3,2,1,0:T(8,128)(2,1)}, bf16[1,2,256,128]{3,2,1,0:T(8,128)(2,1)S(1)}, u32[]{:S(2)}, u32[]{:S(2)}) collective-permute-start(bf16[1,2,256,128]{3,2,1,0:T(8,128)(2,1)} %get-tuple-element.123), channel_id=1, source_target_pairs={{0,24},{4,28},{8,16},{12,20},{16,8},{20,12},{24,0},{28,4},{1,25},{... | collective-permute-start | bytes 393224 | tf_op jit(solution)/shard_map/ppermute | solution.py:233
  146.0 3.2 %collective-permute-start.16 = (bf16[8,4,1,2,64,128]{5,4,3,2,1,0:T(8,128)(2,1)S(1)}, bf16[8,4,1,2,64,128]{5,4,3,2,1,0:T(8,128)(2,1)S(1)}, u32[]{:S(2)}, u32[]{:S(2)}) collective-permute-start(bf16[8,4,1,2,64,128]{5,4,3,2,1,0:T(8,128)(2,1)S(1)} %bitcast.20), channel_id=1, source_target_pairs={{0,4},{4,0},{8,12},{12,8},{16,20},{20,16},{24,28},{28,24},{1,5},{5... | collective-permute-start | bytes 3145736 | tf_op jit(solution)/shard_map/ppermute | solution.py:233
  158.1 4.8 %collective-permute-start.17 = (bf16[1,2,256,128]{3,2,1,0:T(8,128)(2,1)S(1)}, bf16[1,2,256,128]{3,2,1,0:T(8,128)(2,1)S(1)}, u32[]{:S(2)}, u32[]{:S(2)}) collective-permute-start(bf16[1,2,256,128]{3,2,1,0:T(8,128)(2,1)S(1)} %get-tuple-element.142), channel_id=1, source_target_pairs={{0,8},{4,12},{8,0},{12,4},{16,24},{20,28},{24,16},{28,20},{1,9},{5... | collective-permute-start | bytes 393224 | tf_op jit(solution)/shard_map/ppermute | solution.py:233
  158.5 9.7 %collective-permute-start.18 = (bf16[1,2,256,128]{3,2,1,0:T(8,128)(2,1)S(1)}, bf16[1,2,256,128]{3,2,1,0:T(8,128)(2,1)}, u32[]{:S(2)}, u32[]{:S(2)}) collective-permute-start(bf16[1,2,256,128]{3,2,1,0:T(8,128)(2,1)S(1)} %get-tuple-element.143), channel_id=1, source_target_pairs={{0,16},{4,20},{8,24},{12,28},{16,0},{20,4},{24,8},{28,12},{1,17},{... | collective-permute-start | bytes 393224 | tf_op jit(solution)/shard_map/ppermute | solution.py:233
  158.9 9.3 %collective-permute-start.19 = (bf16[1,2,256,128]{3,2,1,0:T(8,128)(2,1)S(1)}, bf16[1,2,256,128]{3,2,1,0:T(8,128)(2,1)}, u32[]{:S(2)}, u32[]{:S(2)}) collective-permute-start(bf16[1,2,256,128]{3,2,1,0:T(8,128)(2,1)S(1)} %get-tuple-element.144), channel_id=1, source_target_pairs={{0,24},{4,28},{8,16},{12,20},{16,8},{20,12},{24,0},{28,4},{1,25},{... | collective-permute-start | bytes 393224 | tf_op jit(solution)/shard_map/ppermute | solution.py:233
  162.2 6.3 %collective-permute-start.21 = (bf16[1,2,256,128]{3,2,1,0:T(8,128)(2,1)S(1)}, bf16[1,2,256,128]{3,2,1,0:T(8,128)(2,1)S(1)}, u32[]{:S(2)}, u32[]{:S(2)}) collective-permute-start(bf16[1,2,256,128]{3,2,1,0:T(8,128)(2,1)S(1)} %get-tuple-element.148), channel_id=1, source_target_pairs={{0,8},{4,12},{8,0},{12,4},{16,24},{20,28},{24,16},{28,20},{1,9},{5... | collective-permute-start | bytes 393224 | tf_op jit(solution)/shard_map/ppermute | solution.py:233
  162.5 7.1 %collective-permute-start.22 = (bf16[1,2,256,128]{3,2,1,0:T(8,128)(2,1)S(1)}, bf16[1,2,256,128]{3,2,1,0:T(8,128)(2,1)S(1)}, u32[]{:S(2)}, u32[]{:S(2)}) collective-permute-start(bf16[1,2,256,128]{3,2,1,0:T(8,128)(2,1)S(1)} %get-tuple-element.149), channel_id=1, source_target_pairs={{0,16},{4,20},{8,24},{12,28},{16,0},{20,4},{24,8},{28,12},{1,17},{... | collective-permute-start | bytes 393224 | tf_op jit(solution)/shard_map/ppermute | solution.py:233
  162.9 8.4 %collective-permute-start.23 = (bf16[1,2,256,128]{3,2,1,0:T(8,128)(2,1)S(1)}, bf16[1,2,256,128]{3,2,1,0:T(8,128)(2,1)S(1)}, u32[]{:S(2)}, u32[]{:S(2)}) collective-permute-start(bf16[1,2,256,128]{3,2,1,0:T(8,128)(2,1)S(1)} %get-tuple-element.150), channel_id=1, source_target_pairs={{0,24},{4,28},{8,16},{12,20},{16,8},{20,12},{24,0},{28,4},{1,25},{... | collective-permute-start | bytes 393224 | tf_op jit(solution)/shard_map/ppermute | solution.py:233
  171.3 3.8 %collective-permute-start.24 = (bf16[8,4,1,2,64,128]{5,4,3,2,1,0:T(8,128)(2,1)S(1)}, bf16[8,4,1,2,64,128]{5,4,3,2,1,0:T(8,128)(2,1)S(1)}, u32[]{:S(2)}, u32[]{:S(2)}) collective-permute-start(bf16[8,4,1,2,64,128]{5,4,3,2,1,0:T(8,128)(2,1)S(1)} %bitcast.18), channel_id=1, source_target_pairs={{0,4},{4,0},{8,12},{12,8},{16,20},{20,16},{24,28},{28,24},{1,5},{5... | collective-permute-start | bytes 3145736 | tf_op jit(solution)/shard_map/ppermute | solution.py:233
  184.3 5.5 %collective-permute-start.25 = (bf16[1,2,256,128]{3,2,1,0:T(8,128)(2,1)S(1)}, bf16[1,2,256,128]{3,2,1,0:T(8,128)(2,1)S(1)}, u32[]{:S(2)}, u32[]{:S(2)}) collective-permute-start(bf16[1,2,256,128]{3,2,1,0:T(8,128)(2,1)S(1)} %get-tuple-element.153), channel_id=1, source_target_pairs={{0,8},{4,12},{8,0},{12,4},{16,24},{20,28},{24,16},{28,20},{1,9},{5... | collective-permute-start | bytes 393224 | tf_op jit(solution)/shard_map/ppermute | solution.py:233
  185.5 8.8 %collective-permute-start.26 = (bf16[1,2,256,128]{3,2,1,0:T(8,128)(2,1)S(1)}, bf16[1,2,256,128]{3,2,1,0:T(8,128)(2,1)S(1)}, u32[]{:S(2)}, u32[]{:S(2)}) collective-permute-start(bf16[1,2,256,128]{3,2,1,0:T(8,128)(2,1)S(1)} %get-tuple-element.154), channel_id=1, source_target_pairs={{0,16},{4,20},{8,24},{12,28},{16,0},{20,4},{24,8},{28,12},{1,17},{... | collective-permute-start | bytes 393224 | tf_op jit(solution)/shard_map/ppermute | solution.py:233
  185.8 8.5 %collective-permute-start.27 = (bf16[1,2,256,128]{3,2,1,0:T(8,128)(2,1)S(1)}, bf16[1,2,256,128]{3,2,1,0:T(8,128)(2,1)S(1)}, u32[]{:S(2)}, u32[]{:S(2)}) collective-permute-start(bf16[1,2,256,128]{3,2,1,0:T(8,128)(2,1)S(1)} %get-tuple-element.155), channel_id=1, source_target_pairs={{0,24},{4,28},{8,16},{12,20},{16,8},{20,12},{24,0},{28,4},{1,25},{... | collective-permute-start | bytes 393224 | tf_op jit(solution)/shard_map/ppermute | solution.py:233
  188.3 6.2 %collective-permute-start.29 = (bf16[1,2,256,128]{3,2,1,0:T(8,128)(2,1)S(1)}, bf16[1,2,256,128]{3,2,1,0:T(8,128)(2,1)S(1)}, u32[]{:S(2)}, u32[]{:S(2)}) collective-permute-start(bf16[1,2,256,128]{3,2,1,0:T(8,128)(2,1)S(1)} %get-tuple-element.159), channel_id=1, source_target_pairs={{0,8},{4,12},{8,0},{12,4},{16,24},{20,28},{24,16},{28,20},{1,9},{5... | collective-permute-start | bytes 393224 | tf_op jit(solution)/shard_map/ppermute | solution.py:233
  189.5 9.6 %collective-permute-start.30 = (bf16[1,2,256,128]{3,2,1,0:T(8,128)(2,1)S(1)}, bf16[1,2,256,128]{3,2,1,0:T(8,128)(2,1)S(1)}, u32[]{:S(2)}, u32[]{:S(2)}) collective-permute-start(bf16[1,2,256,128]{3,2,1,0:T(8,128)(2,1)S(1)} %get-tuple-element.160), channel_id=1, source_target_pairs={{0,16},{4,20},{8,24},{12,28},{16,0},{20,4},{24,8},{28,12},{1,17},{... | collective-permute-start | bytes 393224 | tf_op jit(solution)/shard_map/ppermute | solution.py:233
  189.8 9.2 %collective-permute-start.31 = (bf16[1,2,256,128]{3,2,1,0:T(8,128)(2,1)S(1)}, bf16[1,2,256,128]{3,2,1,0:T(8,128)(2,1)S(1)}, u32[]{:S(2)}, u32[]{:S(2)}) collective-permute-start(bf16[1,2,256,128]{3,2,1,0:T(8,128)(2,1)S(1)} %get-tuple-element.161), channel_id=1, source_target_pairs={{0,24},{4,28},{8,16},{12,20},{16,8},{20,12},{24,0},{28,4},{1,25},{... | collective-permute-start | bytes 393224 | tf_op jit(solution)/shard_map/ppermute | solution.py:233
  (39 other events, 218.2 us)
where the time goes:
time: 207 us; the launch traced here: 203 us
  waiting for transfers between devices  73.3 us (35%)
  Pallas kernels  68.3 us (33%)
  starting transfers between devices  48.6 us (23%)
  local copies, waits for them, and re-layouts  9.47 us (5%)
  other arithmetic  2.36 us (1%)
    ppermute x32, waiting for transfers between devices, exchange(): lax.ppermute(value, 'seq', [(s, s ^ d) for s in range(lax.axis_size('seq'...  44.9 us
    pallas_call x4, Pallas kernels, attention(): pl.pallas_call(functools.partial(attention_kernel, spans, size, group), o...  37 us
    all_to_all x4, waiting for transfers between devices, on_device(): lax.all_to_all(parts, ('seq', 'chan'), split_axis=0, concat_axis=0, tiled...  28.4 us
    ppermute x32, starting transfers between devices, exchange(): lax.ppermute(value, 'seq', [(s, s ^ d) for s in range(lax.axis_size('seq'...  26.2 us
    all_to_all x4, starting transfers between devices, on_device(): lax.all_to_all(parts, ('seq', 'chan'), split_axis=0, concat_axis=0, tiled...  22.4 us
    pallas_call x4, Pallas kernels, pack(): pl.pallas_call(functools.partial(pack_kernel, group, size), grid=(chans,)...  13.7 us
    pallas_call x4, Pallas kernels, unpack(): pl.pallas_call(functools.partial(unpack_kernel, group, size), grid=(rows...  13.2 us
    unnamed x70, local copies, waits for them, and re-layouts  9.01 us
  transfers between devices with their start and end apart: 36, of which 20 were waited for; matrix products, arithmetic and copies ran while one was open for 1% of the time, Pallas kernels for 26%

commit v1 on v0

--- a/solution.py
+++ b/solution.py
@@ -174,7 +174,7 @@
             pltpu.SemaphoreType.DMA((size, group, 3)),
             pltpu.SemaphoreType.DMA((group,)),
         ],
-        compiler_params=pltpu.CompilerParams(vmem_limit_bytes=48 * 1024 * 1024),
+        compiler_params=pltpu.CompilerParams(vmem_limit_bytes=(14 << 20) + 3584 * size * total),
         cost_estimate=pl.CostEstimate(
             flops=12 * HEAD_DIM * pairs,
             bytes_accessed=10 * size * total * HEAD_DIM,
@@ -201,30 +201,37 @@
     )(place, keep, other)
 
 
-def unpack_kernel(group, size, place_ref, *refs):
-    mixed, grads, outs = refs[:group], refs[group : 2 * group], refs[-4:]
+def unpack_kernel(group, size, offset, place_ref, *refs):
+    mixed, grads, outs, sems = refs[:group], refs[group : 2 * group], refs[-5:-1], refs[-1]
+    moves = []
     for d in range(group):
         for j in range(size):
-            head = place_ref[1 + d] * size + j
+            head = (offset * group + place_ref[1 + d]) * size + j
             columns = pl.ds(pl.multiple_of(head * HEAD_DIM, HEAD_DIM), HEAD_DIM)
-            for which in range(2):
-                outs[which][:, columns] = mixed[d][j, which]
-                outs[2 + which][:, columns] = grads[d][j, which]
+            for which in range(4):
+                source = (mixed if which < 2 else grads)[d].at[j, which % 2]
+                moves.append(
+                    pltpu.make_async_copy(
+                        source, outs[which].at[:, columns], sems.at[d, j, which]
+                    )
+                )
+    for move in moves:
+        move.start()
+    for move in moves:
+        move.wait()
 
 
 def unpack(place, mixed, grads, width, offset, held):
     group = len(mixed)
     size, _, rows, _ = mixed[0].shape
-    step = min(rows, 64)
-    return pl.pallas_call(
-        functools.partial(unpack_kernel, group, size),
-        grid=(rows // step,),
+    return pl.pallas_call(
+        functools.partial(unpack_kernel, group, size, offset),
         out_shape=[low_array(rows, width)] * 4,
-        in_specs=[SCALARS]
-        + [pl.BlockSpec((size, 2, step, HEAD_DIM), lambda i: (0, 0, i, 0))] * (2 * group)
-        + [ANYWHERE] * len(held),
-        out_specs=[pl.BlockSpec((step, group * size * HEAD_DIM), lambda i: (i, offset // size))] * 4,
+        in_specs=[SCALARS] + [VECTORS] * (2 * group) + [ANYWHERE] * len(held),
+        out_specs=[ANYWHERE] * 4,
+        scratch_shapes=[pltpu.SemaphoreType.DMA((group, size, 4))],
         input_output_aliases={1 + 2 * group + i: i for i in range(len(held))},
+        compiler_params=pltpu.CompilerParams(vmem_limit_bytes=24 << 20),
         cost_estimate=moved(16 * group * size * rows * HEAD_DIM),
     )(place, *mixed, *grads, *held)
 
@@ -247,16 +254,23 @@
     chips = jnp.bitwise_xor(shard // 2, jnp.arange(group, dtype=jnp.int32))
     place = jnp.concatenate([(shard % 2)[None].astype(jnp.int32), chips])
 
-    gathered = []
-    for chunk in range(heads // group):
-        parts = pack(place, inputs, chans, group, chunk, 1)
-        parts = parts.reshape(shards * chans, 1, 2, rows, HEAD_DIM)
-        mine = lax.all_to_all(parts, ("seq", "chan"), split_axis=0, concat_axis=0, tiled=True)
-        gathered.append(mine.reshape(shards, chans, 1, 2, rows, HEAD_DIM))
-
+    chunks = heads // group
+    parts = [
+        pack(place, inputs, chans, group, chunk, 1).reshape(shards * chans, 1, 2, rows, HEAD_DIM)
+        for chunk in range(chunks)
+    ]
+
+    def gather(part):
+        part = lax.all_to_all(part, ("seq", "chan"), split_axis=0, concat_axis=0, tiled=True)
+        return part.reshape(shards, chans, 1, 2, rows, HEAD_DIM)
+
+    mine = gather(parts[0])
     outs, sent = (), ()
-    for chunk, mine in enumerate(gathered):
-        mine, outs, sent = lax.optimization_barrier((mine, outs, sent))
+    for chunk in range(chunks):
+        later = parts[chunk + 1 :]
+        mine, later, outs, sent = lax.optimization_barrier((mine, later, outs, sent))
+        following = gather(later[0]) if later else None
+        parts[chunk + 1 :] = later
         if chunk > 0:
             outs = unpack(place, *sent, heads * HEAD_DIM, chunk - 1, outs)
         *mixed, keep, send = attention(count, place, start, mine, exchange(mine, 1))
@@ -264,7 +278,8 @@
         grads = add(place, keep, exchange(send, 1))
         grads = [grads[0]] + [exchange(grads[d], 2 * d) for d in range(1, group)]
         sent = (mixed, grads)
-    return tuple(unpack(place, *sent, heads * HEAD_DIM, len(gathered) - 1, outs))
+        mine = following
+    return tuple(unpack(place, *sent, heads * HEAD_DIM, chunks - 1, outs))
 
 
 def solution(mesh):

time: 207 us -> 173 us (0.84)
  waiting for transfers between devices: 73.3 us -> 52.3 us
  Pallas kernels: 68.3 us -> 57.7 us
    all_to_all x4, waiting for transfers between devices: 28.4 us -> 14.3 us  [gather(): lax.all_to_all(part, ('seq', 'chan'), split_axis=0, concat_axis=0, tiled=...]
    ppermute x32, waiting for transfers between devices: 44.9 us -> 38 us  [exchange(): lax.ppermute(value, 'seq', [(s, s ^ d) for s in range(lax.axis_size('seq'...]
    pallas_call x4, Pallas kernels: 13.2 us -> 6.54 us  [unpack(): pl.pallas_call(functools.partial(unpack_kernel, group, size, offset), out...]
    all_to_all x4, starting transfers between devices: 22.4 us -> 20.1 us  [gather(): lax.all_to_all(part, ('seq', 'chan'), split_axis=0, concat_axis=0, tiled=...]
    pallas_call x4, Pallas kernels: 37 us -> 34.8 us  [attention(): pl.pallas_call(functools.partial(attention_kernel, spans, size, group), o...]
    unnamed x70 -> x60, local copies, waits for them, and re-layouts: 9.01 us -> 7.93 us
  transfers between devices with their start and end apart: 36 -> 36, of which waited for: 20 -> 21; matrix products, arithmetic and copies ran while one was open for 1% -> 1% of each run, Pallas kernels for 26% -> 26%
where the time goes in v1:
time: 173 us; the launch traced here: 170 us
  Pallas kernels  57.7 us (33%)
  waiting for transfers between devices  52.3 us (30%)
  starting transfers between devices  48.1 us (28%)
  local copies, waits for them, and re-layouts  8.39 us (5%)
  other arithmetic  2.39 us (1%)
    ppermute x32, waiting for transfers between devices, exchange(): lax.ppermute(value, 'seq', [(s, s ^ d) for s in range(lax.axis_size('seq'...  38 us
    pallas_call x4, Pallas kernels, attention(): pl.pallas_call(functools.partial(attention_kernel, spans, size, group), o...  34.8 us
    ppermute x32, starting transfers between devices, exchange(): lax.ppermute(value, 'seq', [(s, s ^ d) for s in range(lax.axis_size('seq'...  28 us
    all_to_all x4, starting transfers between devices, gather(): lax.all_to_all(part, ('seq', 'chan'), split_axis=0, concat_axis=0, tiled=...  20.1 us
    all_to_all x4, waiting for transfers between devices, gather(): lax.all_to_all(part, ('seq', 'chan'), split_axis=0, concat_axis=0, tiled=...  14.3 us
    pallas_call x4, Pallas kernels, pack(): pl.pallas_call(functools.partial(pack_kernel, group, size), grid=(chans,)...  13.8 us
    unnamed x60, local copies, waits for them, and re-layouts  7.93 us
    pallas_call x4, Pallas kernels, unpack(): pl.pallas_call(functools.partial(unpack_kernel, group, size, offset), out...  6.54 us
  transfers between devices with their start and end apart: 36, of which 21 were waited for; matrix products, arithmetic and copies ran while one was open for 1% of the time, Pallas kernels for 26%

profile of v1, /device:TPU:9, one launch (start us, length us, event | category | flops | bytes accessed | tf_op | source)
XLA Modules:
  0.0 170.2 jit_solution(10642002343077047852)
XLA Ops:
  1.3 3.4 %shard_map.84 = bf16[8,4,1,2,64,128]{5,4,3,2,1,0:T(8,128)(2,1)} custom-call(s32[5]{0:T(128)} %pad_add_fusion.place_ref.refs_1_, bf16[64,8192]{1,0:T(8,128)(2,1)} %refs_0_.7, bf16[64,8192]{1,0:T(8,128)(2,1)} %refs_1_.7, bf16[64,8192]{1,0:T(8,128)(2,1)} %refs_2_.7, bf16[64,8192]{1,0:T(8,128)(2,1)} %refs_3_.7), custom_call_target="tpu_custom_call" | custom-call | bytes 2097152 | tf_op jit(solution)/shard_map/pallas_call | solution.py:57
  4.7 6.4 %all-to-all-start = ((bf16[32,1,2,64,128]{4,3,2,1,0:T(8,128)(2,1)}), bf16[32,1,2,64,128]{4,3,2,1,0:T(8,128)(2,1)S(1)}, u32[]{:S(2)}, u32[]{:S(2)}) async-start(bf16[32,1,2,64,128]{4,3,2,1,0:T(8,128)(2,1)} %bitcast.25), calls=%async_computation | async-start | bytes 2097152 | tf_op jit(solution)/shard_map/all_to_all | solution.py:264
  11.0 3.4 %shard_map.85 = bf16[8,4,1,2,64,128]{5,4,3,2,1,0:T(8,128)(2,1)} custom-call(s32[5]{0:T(128)} %pad_add_fusion.place_ref.refs_1_, bf16[64,8192]{1,0:T(8,128)(2,1)} %refs_0_.7, bf16[64,8192]{1,0:T(8,128)(2,1)} %refs_1_.7, bf16[64,8192]{1,0:T(8,128)(2,1)} %refs_2_.7, bf16[64,8192]{1,0:T(8,128)(2,1)} %refs_3_.7), custom_call_target="tpu_custom_call" | custom-call | bytes 2097152 | tf_op jit(solution)/shard_map/pallas_call | solution.py:57
  14.5 3.5 %shard_map.86 = bf16[8,4,1,2,64,128]{5,4,3,2,1,0:T(8,128)(2,1)} custom-call(s32[5]{0:T(128)} %pad_add_fusion.place_ref.refs_1_, bf16[64,8192]{1,0:T(8,128)(2,1)} %refs_0_.7, bf16[64,8192]{1,0:T(8,128)(2,1)} %refs_1_.7, bf16[64,8192]{1,0:T(8,128)(2,1)} %refs_2_.7, bf16[64,8192]{1,0:T(8,128)(2,1)} %refs_3_.7), custom_call_target="tpu_custom_call" | custom-call | bytes 2097152 | tf_op jit(solution)/shard_map/pallas_call | solution.py:57
  18.0 3.5 %shard_map.87 = bf16[8,4,1,2,64,128]{5,4,3,2,1,0:T(8,128)(2,1)} custom-call(s32[5]{0:T(128)} %pad_add_fusion.place_ref.refs_1_, bf16[64,8192]{1,0:T(8,128)(2,1)} %refs_0_.7, bf16[64,8192]{1,0:T(8,128)(2,1)} %refs_1_.7, bf16[64,8192]{1,0:T(8,128)(2,1)} %refs_2_.7, bf16[64,8192]{1,0:T(8,128)(2,1)} %refs_3_.7), custom_call_target="tpu_custom_call" | custom-call | bytes 2097152 | tf_op jit(solution)/shard_map/pallas_call | solution.py:57
  21.4 14.3 %all-to-all-done = bf16[32,1,2,64,128]{4,3,2,1,0:T(8,128)(2,1)S(1)} async-done(((bf16[32,1,2,64,128]{4,3,2,1,0:T(8,128)(2,1)}), bf16[32,1,2,64,128]{4,3,2,1,0:T(8,128)(2,1)S(1)}, u32[]{:S(2)}, u32[]{:S(2)}) %all-to-all-start) | async-done | bytes 1048608 | tf_op jit(solution)/shard_map/all_to_all | solution.py:264
  35.7 4.8 %all-to-all-start.1 = ((bf16[32,1,2,64,128]{4,3,2,1,0:T(8,128)(2,1)}), bf16[32,1,2,64,128]{4,3,2,1,0:T(8,128)(2,1)S(1)}, u32[]{:S(2)}, u32[]{:S(2)}) async-start(bf16[32,1,2,64,128]{4,3,2,1,0:T(8,128)(2,1)} %bitcast.8), calls=%async_computation.1 | async-start | bytes 2097152 | tf_op jit(solution)/shard_map/all_to_all | solution.py:264
  41.0 1.8 %convert_reduce_fusion = s32[2048]{0:T(1024)S(1)} fusion(s32[2048]{0:T(1024)S(1)} %copy-done.29), kind=kLoop, calls=%fused_computation | loop fusion | flops 12580864 | bytes 16384 | tf_op jit(solution)/shard_map/reduce_sum | solution.py:250
  43.4 8.7 %shard_map.88 = (bf16[1,2,256,128]{3,2,1,0:T(8,128)(2,1)S(1)}, bf16[1,2,256,128]{3,2,1,0:T(8,128)(2,1)S(1)}, bf16[1,2,256,128]{3,2,1,0:T(8,128)(2,1)S(1)}, bf16[...) custom-call(s32[8]{0:T(128)S(1)} %subtract_add_fusion.refs_0_, ...), custom_call_target="tpu_custom_call" | custom-call | flops 1207959552 | bytes 2621440 | tf_op jit(solution)/shard_map/pallas_call | solution.py:159
  60.5 1.7 %collective-permute-start.7 = (bf16[1,2,256,128]{3,2,1,0:T(8,128)(2,1)S(1)}, bf16[1,2,256,128]{3,2,1,0:T(8,128)(2,1)S(1)}, u32[]{:S(2)}, u32[]{:S(2)}) collective-permute-start(bf16[1,2,256,128]{3,2,1,0:T(8,128)(2,1)S(1)} %get-tuple-element.111), channel_id=1, source_target_pairs={{0,24},{4,28},{8,16},{12,20},{16,8},{20,12},{24,0},{28,4},{1,25},{... | collective-permute-start | bytes 393224 | tf_op jit(solution)/shard_map/ppermute | solution.py:240
  62.2 2.5 %collective-permute-done.2.refs_2_ = bf16[1,2,256,128]{3,2,1,0:T(8,128)(2,1)S(1)} collective-permute-done((bf16[1,2,256,128]{3,2,1,0:T(8,128)(2,1)S(1)}, bf16[1,2,256,128]{3,2,1,0:T(8,128)(2,1)S(1)}, u32[]{:S(2)}, u32[]{:S(2)}) %collective-permute-start.2) | collective-permute-done | bytes 131104 | tf_op jit(solution)/shard_map/ppermute | solution.py:240
  69.4 1.4 collective-permute-done.7.refs_7_
  71.4 5.0 %all-to-all-start.2 = ((bf16[32,1,2,64,128]{4,3,2,1,0:T(8,128)(2,1)}), bf16[32,1,2,64,128]{4,3,2,1,0:T(8,128)(2,1)S(1)}, u32[]{:S(2)}, u32[]{:S(2)}) async-start(bf16[32,1,2,64,128]{4,3,2,1,0:T(8,128)(2,1)} %bitcast.24), calls=%async_computation.2 | async-start | bytes 2097152 | tf_op jit(solution)/shard_map/all_to_all | solution.py:264
  76.8 2.3 %collective-permute-done.8.refs_4_ = bf16[8,4,1,2,64,128]{5,4,3,2,1,0:T(8,128)(2,1)S(1)} collective-permute-done((bf16[8,4,1,2,64,128]{5,4,3,2,1,0:T(8,128)(2,1)S(1)}, bf16[8,4,1,2,64,128]{5,4,3,2,1,0:T(8,128)(2,1)S(1)}, u32[]{:S(2)}, u32[]{:S(2)}) %collective-permute-start.8) | collective-permute-done | bytes 1048608 | tf_op jit(solution)/shard_map/ppermute | solution.py:240
  79.1 8.6 %shard_map.91 = (bf16[1,2,256,128]{3,2,1,0:T(8,128)(2,1)S(1)}, bf16[1,2,256,128]{3,2,1,0:T(8,128)(2,1)S(1)}, bf16[1,2,256,128]{3,2,1,0:T(8,128)(2,1)S(1)}, bf16[...) custom-call(s32[8]{0:T(128)S(1)} %subtract_add_fusion.refs_0_, ...), custom_call_target="tpu_custom_call" | custom-call | flops 1207959552 | bytes 2621440 | tf_op jit(solution)/shard_map/pallas_call | solution.py:159
  93.7 6.4 %collective-permute-done.10.refs_2_ = bf16[1,2,256,128]{3,2,1,0:T(8,128)(2,1)S(1)} collective-permute-done((bf16[1,2,256,128]{3,2,1,0:T(8,128)(2,1)S(1)}, bf16[1,2,256,128]{3,2,1,0:T(8,128)(2,1)S(1)}, u32[]{:S(2)}, u32[]{:S(2)}) %collective-permute-start.10) | collective-permute-done | bytes 131104 | tf_op jit(solution)/shard_map/ppermute | solution.py:240
  100.9 1.6 shard_map.90
  104.6 2.5 %collective-permute-done.15.refs_7_ = bf16[1,2,256,128]{3,2,1,0:T(8,128)(2,1)S(1)} collective-permute-done((bf16[1,2,256,128]{3,2,1,0:T(8,128)(2,1)S(1)}, bf16[1,2,256,128]{3,2,1,0:T(8,128)(2,1)S(1)}, u32[]{:S(2)}, u32[]{:S(2)}) %collective-permute-start.15) | collective-permute-done | bytes 131104 | tf_op jit(solution)/shard_map/ppermute | solution.py:240
  107.8 4.0 %all-to-all-start.3 = ((bf16[32,1,2,64,128]{4,3,2,1,0:T(8,128)(2,1)}), bf16[32,1,2,64,128]{4,3,2,1,0:T(8,128)(2,1)S(1)}, u32[]{:S(2)}, u32[]{:S(2)}) async-start(bf16[32,1,2,64,128]{4,3,2,1,0:T(8,128)(2,1)} %bitcast.23), calls=%async_computation.3 | async-start | bytes 2097152 | tf_op jit(solution)/shard_map/all_to_all | solution.py:264
  112.2 2.3 %collective-permute-done.16.refs_4_ = bf16[8,4,1,2,64,128]{5,4,3,2,1,0:T(8,128)(2,1)S(1)} collective-permute-done((bf16[8,4,1,2,64,128]{5,4,3,2,1,0:T(8,128)(2,1)S(1)}, bf16[8,4,1,2,64,128]{5,4,3,2,1,0:T(8,128)(2,1)S(1)}, u32[]{:S(2)}, u32[]{:S(2)}) %collective-permute-start.16) | collective-permute-done | bytes 1048608 | tf_op jit(solution)/shard_map/ppermute | solution.py:240
  114.5 8.6 %shard_map.94 = (bf16[1,2,256,128]{3,2,1,0:T(8,128)(2,1)S(1)}, bf16[1,2,256,128]{3,2,1,0:T(8,128)(2,1)S(1)}, bf16[1,2,256,128]{3,2,1,0:T(8,128)(2,1)S(1)}, bf16[...) custom-call(s32[8]{0:T(128)S(1)} %subtract_add_fusion.refs_0_, ...), custom_call_target="tpu_custom_call" | custom-call | flops 1207959552 | bytes 2621440 | tf_op jit(solution)/shard_map/pallas_call | solution.py:159
  130.3 2.3 %collective-permute-start.23 = (bf16[1,2,256,128]{3,2,1,0:T(8,128)(2,1)S(1)}, bf16[1,2,256,128]{3,2,1,0:T(8,128)(2,1)S(1)}, u32[]{:S(2)}, u32[]{:S(2)}) collective-permute-start(bf16[1,2,256,128]{3,2,1,0:T(8,128)(2,1)S(1)} %get-tuple-element.164), channel_id=1, source_target_pairs={{0,24},{4,28},{8,16},{12,20},{16,8},{20,12},{24,0},{28,4},{1,25},{... | collective-permute-start | bytes 393224 | tf_op jit(solution)/shard_map/ppermute | solution.py:240
  132.6 1.6 shard_map.93
  134.7 2.9 %collective-permute-done.21.refs_5_ = bf16[1,2,256,128]{3,2,1,0:T(8,128)(2,1)S(1)} collective-permute-done((bf16[1,2,256,128]{3,2,1,0:T(8,128)(2,1)S(1)}, bf16[1,2,256,128]{3,2,1,0:T(8,128)(2,1)S(1)}, u32[]{:S(2)}, u32[]{:S(2)}) %collective-permute-start.21) | collective-permute-done | bytes 131104 | tf_op jit(solution)/shard_map/ppermute | solution.py:240
  138.5 2.9 %collective-permute-done.23.refs_7_ = bf16[1,2,256,128]{3,2,1,0:T(8,128)(2,1)S(1)} collective-permute-done((bf16[1,2,256,128]{3,2,1,0:T(8,128)(2,1)S(1)}, bf16[1,2,256,128]{3,2,1,0:T(8,128)(2,1)S(1)}, u32[]{:S(2)}, u32[]{:S(2)}) %collective-permute-start.23) | collective-permute-done | bytes 131104 | tf_op jit(solution)/shard_map/ppermute | solution.py:240
  142.4 2.3 %collective-permute-done.24.refs_4_ = bf16[8,4,1,2,64,128]{5,4,3,2,1,0:T(8,128)(2,1)S(1)} collective-permute-done((bf16[8,4,1,2,64,128]{5,4,3,2,1,0:T(8,128)(2,1)S(1)}, bf16[8,4,1,2,64,128]{5,4,3,2,1,0:T(8,128)(2,1)S(1)}, u32[]{:S(2)}, u32[]{:S(2)}) %collective-permute-start.24) | collective-permute-done | bytes 1048608 | tf_op jit(solution)/shard_map/ppermute | solution.py:240
  144.7 8.9 %shard_map.96 = (bf16[1,2,256,128]{3,2,1,0:T(8,128)(2,1)S(1)}, bf16[1,2,256,128]{3,2,1,0:T(8,128)(2,1)S(1)}, bf16[1,2,256,128]{3,2,1,0:T(8,128)(2,1)S(1)}, bf16[...) custom-call(s32[8]{0:T(128)S(1)} %subtract_add_fusion.refs_0_, ...), custom_call_target="tpu_custom_call" | custom-call | flops 1207959552 | bytes 2621440 | tf_op jit(solution)/shard_map/pallas_call | solution.py:159
  157.0 1.4 collective-permute-start.29
  159.7 1.6 shard_map.98
  161.8 2.0 %collective-permute-done.29.refs_5_ = bf16[1,2,256,128]{3,2,1,0:T(8,128)(2,1)S(1)} collective-permute-done((bf16[1,2,256,128]{3,2,1,0:T(8,128)(2,1)S(1)}, bf16[1,2,256,128]{3,2,1,0:T(8,128)(2,1)S(1)}, u32[]{:S(2)}, u32[]{:S(2)}) %collective-permute-start.29) | collective-permute-done | bytes 131104 | tf_op jit(solution)/shard_map/ppermute | solution.py:240
  163.7 4.6 %collective-permute-done.30.refs_6_ = bf16[1,2,256,128]{3,2,1,0:T(8,128)(2,1)S(1)} collective-permute-done((bf16[1,2,256,128]{3,2,1,0:T(8,128)(2,1)S(1)}, bf16[1,2,256,128]{3,2,1,0:T(8,128)(2,1)S(1)}, u32[]{:S(2)}, u32[]{:S(2)}) %collective-permute-start.30) | collective-permute-done | bytes 131104 | tf_op jit(solution)/shard_map/ppermute | solution.py:240
  168.3 1.6 shard_map.99
  (122 shorter events, 40.1 us)
Async XLA Ops:
  4.7 31.1 %all-to-all-start = ((bf16[32,1,2,64,128]{4,3,2,1,0:T(8,128)(2,1)}), bf16[32,1,2,64,128]{4,3,2,1,0:T(8,128)(2,1)S(1)}, u32[]{:S(2)}, u32[]{:S(2)}) async-start(bf16[32,1,2,64,128]{4,3,2,1,0:T(8,128)(2,1)} %bitcast.25), calls=%async_computation | async-start | bytes 2097152 | tf_op jit(solution)/shard_map/all_to_all | solution.py:264
  35.7 35.6 %all-to-all-start.1 = ((bf16[32,1,2,64,128]{4,3,2,1,0:T(8,128)(2,1)}), bf16[32,1,2,64,128]{4,3,2,1,0:T(8,128)(2,1)S(1)}, u32[]{:S(2)}, u32[]{:S(2)}) async-start(bf16[32,1,2,64,128]{4,3,2,1,0:T(8,128)(2,1)} %bitcast.8), calls=%async_computation.1 | async-start | bytes 2097152 | tf_op jit(solution)/shard_map/all_to_all | solution.py:264
  40.6 2.9 %collective-permute-start = (bf16[8,4,1,2,64,128]{5,4,3,2,1,0:T(8,128)(2,1)S(1)}, bf16[8,4,1,2,64,128]{5,4,3,2,1,0:T(8,128)(2,1)}, u32[]{:S(2)}, u32[]{:S(2)}) collective-permute-start(bf16[8,4,1,2,64,128]{5,4,3,2,1,0:T(8,128)(2,1)S(1)} %bitcast.21), channel_id=1, source_target_pairs={{0,4},{4,0},{8,12},{12,8},{16,20},{20,16},{24,28},{28,24},{1,5},{5... | collective-permute-start | bytes 3145736 | tf_op jit(solution)/shard_map/ppermute | solution.py:240
  52.8 7.0 %collective-permute-start.1 = (bf16[1,2,256,128]{3,2,1,0:T(8,128)(2,1)S(1)}, bf16[1,2,256,128]{3,2,1,0:T(8,128)(2,1)S(1)}, u32[]{:S(2)}, u32[]{:S(2)}) collective-permute-start(bf16[1,2,256,128]{3,2,1,0:T(8,128)(2,1)S(1)} %get-tuple-element.103), channel_id=1, source_target_pairs={{0,8},{4,12},{8,0},{12,4},{16,24},{20,28},{24,16},{28,20},{1,9},{5... | collective-permute-start | bytes 393224 | tf_op jit(solution)/shard_map/ppermute | solution.py:240
  54.0 10.7 %collective-permute-start.2 = (bf16[1,2,256,128]{3,2,1,0:T(8,128)(2,1)S(1)}, bf16[1,2,256,128]{3,2,1,0:T(8,128)(2,1)S(1)}, u32[]{:S(2)}, u32[]{:S(2)}) collective-permute-start(bf16[1,2,256,128]{3,2,1,0:T(8,128)(2,1)S(1)} %get-tuple-element.104), channel_id=1, source_target_pairs={{0,16},{4,20},{8,24},{12,28},{16,0},{20,4},{24,8},{28,12},{1,17},{... | collective-permute-start | bytes 393224 | tf_op jit(solution)/shard_map/ppermute | solution.py:240
  55.2 10.2 %collective-permute-start.3 = (bf16[1,2,256,128]{3,2,1,0:T(8,128)(2,1)S(1)}, bf16[1,2,256,128]{3,2,1,0:T(8,128)(2,1)S(1)}, u32[]{:S(2)}, u32[]{:S(2)}) collective-permute-start(bf16[1,2,256,128]{3,2,1,0:T(8,128)(2,1)S(1)} %get-tuple-element.105), channel_id=1, source_target_pairs={{0,24},{4,28},{8,16},{12,20},{16,8},{20,12},{24,0},{28,4},{1,25},{... | collective-permute-start | bytes 393224 | tf_op jit(solution)/shard_map/ppermute | solution.py:240
  56.7 10.2 %collective-permute-start.5 = (bf16[1,2,256,128]{3,2,1,0:T(8,128)(2,1)S(1)}, bf16[1,2,256,128]{3,2,1,0:T(8,128)(2,1)S(1)}, u32[]{:S(2)}, u32[]{:S(2)}) collective-permute-start(bf16[1,2,256,128]{3,2,1,0:T(8,128)(2,1)S(1)} %get-tuple-element.109), channel_id=1, source_target_pairs={{0,8},{4,12},{8,0},{12,4},{16,24},{20,28},{24,16},{28,20},{1,9},{5... | collective-permute-start | bytes 393224 | tf_op jit(solution)/shard_map/ppermute | solution.py:240
  57.9 10.8 %collective-permute-start.6 = (bf16[1,2,256,128]{3,2,1,0:T(8,128)(2,1)S(1)}, bf16[1,2,256,128]{3,2,1,0:T(8,128)(2,1)S(1)}, u32[]{:S(2)}, u32[]{:S(2)}) collective-permute-start(bf16[1,2,256,128]{3,2,1,0:T(8,128)(2,1)S(1)} %get-tuple-element.110), channel_id=1, source_target_pairs={{0,16},{4,20},{8,24},{12,28},{16,0},{20,4},{24,8},{28,12},{1,17},{... | collective-permute-start | bytes 393224 | tf_op jit(solution)/shard_map/ppermute | solution.py:240
  60.5 10.3 %collective-permute-start.7 = (bf16[1,2,256,128]{3,2,1,0:T(8,128)(2,1)S(1)}, bf16[1,2,256,128]{3,2,1,0:T(8,128)(2,1)S(1)}, u32[]{:S(2)}, u32[]{:S(2)}) collective-permute-start(bf16[1,2,256,128]{3,2,1,0:T(8,128)(2,1)S(1)} %get-tuple-element.111), channel_id=1, source_target_pairs={{0,24},{4,28},{8,16},{12,20},{16,8},{20,12},{24,0},{28,4},{1,25},{... | collective-permute-start | bytes 393224 | tf_op jit(solution)/shard_map/ppermute | solution.py:240
  71.4 36.4 %all-to-all-start.2 = ((bf16[32,1,2,64,128]{4,3,2,1,0:T(8,128)(2,1)}), bf16[32,1,2,64,128]{4,3,2,1,0:T(8,128)(2,1)S(1)}, u32[]{:S(2)}, u32[]{:S(2)}) async-start(bf16[32,1,2,64,128]{4,3,2,1,0:T(8,128)(2,1)} %bitcast.24), calls=%async_computation.2 | async-start | bytes 2097152 | tf_op jit(solution)/shard_map/all_to_all | solution.py:264
  87.8 2.8 %collective-permute-start.12 = (bf16[4,1,2,256,128]{4,3,2,1,0:T(8,128)(2,1)S(1)}, bf16[4,1,2,256,128]{4,3,2,1,0:T(8,128)(2,1)S(1)}, u32[]{:S(2)}, u32[]{:S(2)}) collective-permute-start(bf16[4,1,2,256,128]{4,3,2,1,0:T(8,128)(2,1)S(1)} %get-tuple-element.132), channel_id=1, source_target_pairs={{0,4},{4,0},{8,12},{12,8},{16,20},{20,16},{24,28},{28,24},{1,5},{5... | collective-permute-start | bytes 1572872 | tf_op jit(solution)/shard_map/ppermute | solution.py:240
  87.9 12.2 %collective-permute-start.10 = (bf16[1,2,256,128]{3,2,1,0:T(8,128)(2,1)S(1)}, bf16[1,2,256,128]{3,2,1,0:T(8,128)(2,1)S(1)}, u32[]{:S(2)}, u32[]{:S(2)}) collective-permute-start(bf16[1,2,256,128]{3,2,1,0:T(8,128)(2,1)S(1)} %get-tuple-element.129), channel_id=1, source_target_pairs={{0,16},{4,20},{8,24},{12,28},{16,0},{20,4},{24,8},{28,12},{1,17},{... | collective-permute-start | bytes 393224 | tf_op jit(solution)/shard_map/ppermute | solution.py:240
  89.1 13.4 %collective-permute-start.11 = (bf16[1,2,256,128]{3,2,1,0:T(8,128)(2,1)S(1)}, bf16[1,2,256,128]{3,2,1,0:T(8,128)(2,1)S(1)}, u32[]{:S(2)}, u32[]{:S(2)}) collective-permute-start(bf16[1,2,256,128]{3,2,1,0:T(8,128)(2,1)S(1)} %get-tuple-element.130), channel_id=1, source_target_pairs={{0,24},{4,28},{8,16},{12,20},{16,8},{20,12},{24,0},{28,4},{1,25},{... | collective-permute-start | bytes 393224 | tf_op jit(solution)/shard_map/ppermute | solution.py:240
  90.3 12.2 %collective-permute-start.9 = (bf16[1,2,256,128]{3,2,1,0:T(8,128)(2,1)S(1)}, bf16[1,2,256,128]{3,2,1,0:T(8,128)(2,1)S(1)}, u32[]{:S(2)}, u32[]{:S(2)}) collective-permute-start(bf16[1,2,256,128]{3,2,1,0:T(8,128)(2,1)S(1)} %get-tuple-element.128), channel_id=1, source_target_pairs={{0,8},{4,12},{8,0},{12,4},{16,24},{20,28},{24,16},{28,20},{1,9},{5... | collective-permute-start | bytes 393224 | tf_op jit(solution)/shard_map/ppermute | solution.py:240
  91.3 12.1 %collective-permute-start.13 = (bf16[1,2,256,128]{3,2,1,0:T(8,128)(2,1)S(1)}, bf16[1,2,256,128]{3,2,1,0:T(8,128)(2,1)S(1)}, u32[]{:S(2)}, u32[]{:S(2)}) collective-permute-start(bf16[1,2,256,128]{3,2,1,0:T(8,128)(2,1)S(1)} %get-tuple-element.134), channel_id=1, source_target_pairs={{0,8},{4,12},{8,0},{12,4},{16,24},{20,28},{24,16},{28,20},{1,9},{5... | collective-permute-start | bytes 393224 | tf_op jit(solution)/shard_map/ppermute | solution.py:240
  92.5 11.5 %collective-permute-start.14 = (bf16[1,2,256,128]{3,2,1,0:T(8,128)(2,1)S(1)}, bf16[1,2,256,128]{3,2,1,0:T(8,128)(2,1)S(1)}, u32[]{:S(2)}, u32[]{:S(2)}) collective-permute-start(bf16[1,2,256,128]{3,2,1,0:T(8,128)(2,1)S(1)} %get-tuple-element.135), channel_id=1, source_target_pairs={{0,16},{4,20},{8,24},{12,28},{16,0},{20,4},{24,8},{28,12},{1,17},{... | collective-permute-start | bytes 393224 | tf_op jit(solution)/shard_map/ppermute | solution.py:240
  100.1 7.0 %collective-permute-start.15 = (bf16[1,2,256,128]{3,2,1,0:T(8,128)(2,1)S(1)}, bf16[1,2,256,128]{3,2,1,0:T(8,128)(2,1)S(1)}, u32[]{:S(2)}, u32[]{:S(2)}) collective-permute-start(bf16[1,2,256,128]{3,2,1,0:T(8,128)(2,1)S(1)} %get-tuple-element.136), channel_id=1, source_target_pairs={{0,24},{4,28},{8,16},{12,20},{16,8},{20,12},{24,0},{28,4},{1,25},{... | collective-permute-start | bytes 393224 | tf_op jit(solution)/shard_map/ppermute | solution.py:240
  107.8 33.5 %all-to-all-start.3 = ((bf16[32,1,2,64,128]{4,3,2,1,0:T(8,128)(2,1)}), bf16[32,1,2,64,128]{4,3,2,1,0:T(8,128)(2,1)S(1)}, u32[]{:S(2)}, u32[]{:S(2)}) async-start(bf16[32,1,2,64,128]{4,3,2,1,0:T(8,128)(2,1)} %bitcast.23), calls=%async_computation.3 | async-start | bytes 2097152 | tf_op jit(solution)/shard_map/all_to_all | solution.py:264
  123.2 7.0 %collective-permute-start.17 = (bf16[1,2,256,128]{3,2,1,0:T(8,128)(2,1)S(1)}, bf16[1,2,256,128]{3,2,1,0:T(8,128)(2,1)S(1)}, u32[]{:S(2)}, u32[]{:S(2)}) collective-permute-start(bf16[1,2,256,128]{3,2,1,0:T(8,128)(2,1)S(1)} %get-tuple-element.156), channel_id=1, source_target_pairs={{0,8},{4,12},{8,0},{12,4},{16,24},{20,28},{24,16},{28,20},{1,9},{5... | collective-permute-start | bytes 393224 | tf_op jit(solution)/shard_map/ppermute | solution.py:240
  124.5 9.8 %collective-permute-start.18 = (bf16[1,2,256,128]{3,2,1,0:T(8,128)(2,1)S(1)}, bf16[1,2,256,128]{3,2,1,0:T(8,128)(2,1)S(1)}, u32[]{:S(2)}, u32[]{:S(2)}) collective-permute-start(bf16[1,2,256,128]{3,2,1,0:T(8,128)(2,1)S(1)} %get-tuple-element.157), channel_id=1, source_target_pairs={{0,16},{4,20},{8,24},{12,28},{16,0},{20,4},{24,8},{28,12},{1,17},{... | collective-permute-start | bytes 393224 | tf_op jit(solution)/shard_map/ppermute | solution.py:240
  125.7 9.0 %collective-permute-start.19 = (bf16[1,2,256,128]{3,2,1,0:T(8,128)(2,1)S(1)}, bf16[1,2,256,128]{3,2,1,0:T(8,128)(2,1)S(1)}, u32[]{:S(2)}, u32[]{:S(2)}) collective-permute-start(bf16[1,2,256,128]{3,2,1,0:T(8,128)(2,1)S(1)} %get-tuple-element.158), channel_id=1, source_target_pairs={{0,24},{4,28},{8,16},{12,20},{16,8},{20,12},{24,0},{28,4},{1,25},{... | collective-permute-start | bytes 393224 | tf_op jit(solution)/shard_map/ppermute | solution.py:240
  126.6 11.0 %collective-permute-start.21 = (bf16[1,2,256,128]{3,2,1,0:T(8,128)(2,1)S(1)}, bf16[1,2,256,128]{3,2,1,0:T(8,128)(2,1)S(1)}, u32[]{:S(2)}, u32[]{:S(2)}) collective-permute-start(bf16[1,2,256,128]{3,2,1,0:T(8,128)(2,1)S(1)} %get-tuple-element.162), channel_id=1, source_target_pairs={{0,8},{4,12},{8,0},{12,4},{16,24},{20,28},{24,16},{28,20},{1,9},{5... | collective-permute-start | bytes 393224 | tf_op jit(solution)/shard_map/ppermute | solution.py:240
  127.8 10.6 %collective-permute-start.22 = (bf16[1,2,256,128]{3,2,1,0:T(8,128)(2,1)S(1)}, bf16[1,2,256,128]{3,2,1,0:T(8,128)(2,1)S(1)}, u32[]{:S(2)}, u32[]{:S(2)}) collective-permute-start(bf16[1,2,256,128]{3,2,1,0:T(8,128)(2,1)S(1)} %get-tuple-element.163), channel_id=1, source_target_pairs={{0,16},{4,20},{8,24},{12,28},{16,0},{20,4},{24,8},{28,12},{1,17},{... | collective-permute-start | bytes 393224 | tf_op jit(solution)/shard_map/ppermute | solution.py:240
  130.3 11.1 %collective-permute-start.23 = (bf16[1,2,256,128]{3,2,1,0:T(8,128)(2,1)S(1)}, bf16[1,2,256,128]{3,2,1,0:T(8,128)(2,1)S(1)}, u32[]{:S(2)}, u32[]{:S(2)}) collective-permute-start(bf16[1,2,256,128]{3,2,1,0:T(8,128)(2,1)S(1)} %get-tuple-element.164), channel_id=1, source_target_pairs={{0,24},{4,28},{8,16},{12,20},{16,8},{20,12},{24,0},{28,4},{1,25},{... | collective-permute-start | bytes 393224 | tf_op jit(solution)/shard_map/ppermute | solution.py:240
  141.3 3.4 %collective-permute-start.24 = (bf16[8,4,1,2,64,128]{5,4,3,2,1,0:T(8,128)(2,1)S(1)}, bf16[8,4,1,2,64,128]{5,4,3,2,1,0:T(8,128)(2,1)S(1)}, u32[]{:S(2)}, u32[]{:S(2)}) collective-permute-start(bf16[8,4,1,2,64,128]{5,4,3,2,1,0:T(8,128)(2,1)S(1)} %bitcast.15), channel_id=1, source_target_pairs={{0,4},{4,0},{8,12},{12,8},{16,20},{20,16},{24,28},{28,24},{1,5},{5... | collective-permute-start | bytes 3145736 | tf_op jit(solution)/shard_map/ppermute | solution.py:240
  153.6 2.8 %collective-permute-start.28 = (bf16[4,1,2,256,128]{4,3,2,1,0:T(8,128)(2,1)S(1)}, bf16[4,1,2,256,128]{4,3,2,1,0:T(8,128)(2,1)S(1)}, u32[]{:S(2)}, u32[]{:S(2)}) collective-permute-start(bf16[4,1,2,256,128]{4,3,2,1,0:T(8,128)(2,1)S(1)} %get-tuple-element.171), channel_id=1, source_target_pairs={{0,4},{4,0},{8,12},{12,8},{16,20},{20,16},{24,28},{28,24},{1,5},{5... | collective-permute-start | bytes 1572872 | tf_op jit(solution)/shard_map/ppermute | solution.py:240
  153.7 5.0 %collective-permute-start.25 = (bf16[1,2,256,128]{3,2,1,0:T(8,128)(2,1)S(1)}, bf16[1,2,256,128]{3,2,1,0:T(8,128)(2,1)S(1)}, u32[]{:S(2)}, u32[]{:S(2)}) collective-permute-start(bf16[1,2,256,128]{3,2,1,0:T(8,128)(2,1)S(1)} %get-tuple-element.167), channel_id=1, source_target_pairs={{0,8},{4,12},{8,0},{12,4},{16,24},{20,28},{24,16},{28,20},{1,9},{5... | collective-permute-start | bytes 393224 | tf_op jit(solution)/shard_map/ppermute | solution.py:240
  155.0 6.4 %collective-permute-start.26 = (bf16[1,2,256,128]{3,2,1,0:T(8,128)(2,1)S(1)}, bf16[1,2,256,128]{3,2,1,0:T(8,128)(2,1)S(1)}, u32[]{:S(2)}, u32[]{:S(2)}) collective-permute-start(bf16[1,2,256,128]{3,2,1,0:T(8,128)(2,1)S(1)} %get-tuple-element.168), channel_id=1, source_target_pairs={{0,16},{4,20},{8,24},{12,28},{16,0},{20,4},{24,8},{28,12},{1,17},{... | collective-permute-start | bytes 393224 | tf_op jit(solution)/shard_map/ppermute | solution.py:240
  155.3 6.5 %collective-permute-start.27 = (bf16[1,2,256,128]{3,2,1,0:T(8,128)(2,1)S(1)}, bf16[1,2,256,128]{3,2,1,0:T(8,128)(2,1)S(1)}, u32[]{:S(2)}, u32[]{:S(2)}) collective-permute-start(bf16[1,2,256,128]{3,2,1,0:T(8,128)(2,1)S(1)} %get-tuple-element.169), channel_id=1, source_target_pairs={{0,24},{4,28},{8,16},{12,20},{16,8},{20,12},{24,0},{28,4},{1,25},{... | collective-permute-start | bytes 393224 | tf_op jit(solution)/shard_map/ppermute | solution.py:240
  157.0 6.7 %collective-permute-start.29 = (bf16[1,2,256,128]{3,2,1,0:T(8,128)(2,1)S(1)}, bf16[1,2,256,128]{3,2,1,0:T(8,128)(2,1)S(1)}, u32[]{:S(2)}, u32[]{:S(2)}) collective-permute-start(bf16[1,2,256,128]{3,2,1,0:T(8,128)(2,1)S(1)} %get-tuple-element.173), channel_id=1, source_target_pairs={{0,8},{4,12},{8,0},{12,4},{16,24},{20,28},{24,16},{28,20},{1,9},{5... | collective-permute-start | bytes 393224 | tf_op jit(solution)/shard_map/ppermute | solution.py:240
  158.4 10.0 %collective-permute-start.30 = (bf16[1,2,256,128]{3,2,1,0:T(8,128)(2,1)S(1)}, bf16[1,2,256,128]{3,2,1,0:T(8,128)(2,1)S(1)}, u32[]{:S(2)}, u32[]{:S(2)}) collective-permute-start(bf16[1,2,256,128]{3,2,1,0:T(8,128)(2,1)S(1)} %get-tuple-element.174), channel_id=1, source_target_pairs={{0,16},{4,20},{8,24},{12,28},{16,0},{20,4},{24,8},{28,12},{1,17},{... | collective-permute-start | bytes 393224 | tf_op jit(solution)/shard_map/ppermute | solution.py:240
  158.7 9.7 %collective-permute-start.31 = (bf16[1,2,256,128]{3,2,1,0:T(8,128)(2,1)S(1)}, bf16[1,2,256,128]{3,2,1,0:T(8,128)(2,1)S(1)}, u32[]{:S(2)}, u32[]{:S(2)}) collective-permute-start(bf16[1,2,256,128]{3,2,1,0:T(8,128)(2,1)S(1)} %get-tuple-element.175), channel_id=1, source_target_pairs={{0,24},{4,28},{8,16},{12,20},{16,8},{20,12},{24,0},{28,4},{1,25},{... | collective-permute-start | bytes 393224 | tf_op jit(solution)/shard_map/ppermute | solution.py:240
  (34 other events, 206.2 us)
